TPU v7x, 128 devices: a whole 4x4x4 slice. The times are simulated.
128 devices in a mesh: frames: 32 (over z, x, core), rows: 4 (over y).
Axes of the slice: x: 4, y: 4, z: 4, core: 2. Of those that a mesh axis runs over, the one named last changes fastest.
Arguments:
- latents: bfloat16 [256, 8, 128, 512], P('frames', 'rows'), may hold values from -6 to 6
- gain_one: float32 [512], replicated, may hold values from 0.1 to 1.9
- spatial_weight: bfloat16 [3, 3, 512, 512], replicated, may hold values from -0.09375 to 0.09375
- gain_two: float32 [512], replicated, may hold values from 0.1 to 1.9
- temporal_weight: bfloat16 [3, 512, 512], replicated, may hold values from -0.15625 to 0.15625
- gain_three: float32 [512], replicated, may hold values from 0.1 to 1.9
- query_weight: bfloat16 [512, 512], replicated, as said below
- key_weight: bfloat16 [512, 512], replicated, as said below
- value_weight: bfloat16 [512, 512], replicated, may hold values from -0.25 to 0.25
- out_weight: bfloat16 [512, 512], replicated, may hold values from -0.25 to 0.25
Outputs:
- tokens: bfloat16 [262144, 512], P(('frames', 'rows'))
Inputs may be any that keep to these rules, and one draw needn't show every extreme that they name: `query_weight`: a projection matrix with entries of order 512 ** -0.5 or larger. `key_weight`: a projection matrix with entries of order 512 ** -0.5.
All inputs are finite; a program needn't handle non-finite values.
Results may differ from a plain program's by a relative error of at most 0.014.
Values may be sent and summed in bfloat16 or wider, within the bound.
No kernel may reach another device: no remote copies, remote signals or barrier semaphores. Data moves between devices by JAX's collectives and lax.ppermute only.
A program may use at most 128 MiB of HBM per device.

v0:
```python
import functools

import jax
import jax.numpy as jnp
from jax import lax
from jax.experimental import pallas as pl
from jax.experimental.pallas import tpu as pltpu
from jax.sharding import PartitionSpec as P

C = 512
HEADS = 8
HD = 64
W = 128
NF = 16
RIM = 8
EDGE = 2
MAIN = 8 - EDGE
CUTS = (0, 64, 128)
ORDER = ("e0", "i0", "s0", "t0", "i1", "s1", "t1", "p0", "p1", "a0", "w0", "a1", "w1")
AXES = ("frames", "rows")
F32 = jnp.float32
BF16 = jnp.bfloat16
HBM = pl.BlockSpec(memory_space=pltpu.HBM)
SMEM = pl.BlockSpec(memory_space=pltpu.SMEM)
VMEM = pl.BlockSpec(memory_space=pltpu.VMEM)


def routed(x, route):
    frames, rows = lax.axis_size("frames"), lax.axis_size("rows")
    pairs = []
    for f in range(frames):
        for r in range(rows):
            to_f, to_r = route(f, r)
            pairs.append((f * rows + r, to_f % frames * rows + to_r % rows))
    return lax.ppermute(x, AXES, pairs)


def to_sibling(f, r):
    return f ^ 1, r


def to_same_core(f, r):
    return f, (r + 1 if f % 2 == 0 else r - 1)


def to_other_core(f, r):
    return f ^ 1, (r + 1 if f % 2 == 1 else r - 1)


def to_next_chip(f, r):
    return f + 2, r


def pass_on(info, info_out):
    for i in range(4):
        info_out[i] = info[i]


INFO = jax.ShapeDtypeStruct((4,), jnp.int32)


def rms(v, gain):
    mean_square = jnp.mean(v * v, axis=-1, keepdims=True)
    return v * lax.rsqrt(mean_square + 1e-06) * gain


def mm(a, b):
    return jnp.dot(a, b, preferred_element_type=F32)


def piece_bounds(j):
    lo = 0 if j == 0 else CUTS[j] + RIM
    hi = W if j == len(CUTS) - 2 else CUTS[j + 1] + RIM
    return lo, hi


def frames_per_step(count, wc, rows):
    step = max(1, rows // wc)
    while count % step:
        step -= 1
    return step


def window(j):
    c0, c1 = CUTS[j], CUTS[j + 1]
    return c0, c1, max(c0 - 8, 0), min(c1 + 8, W)


def shifted_into(dst, rows, v, bounds):
    c0, c1, lo, hi = bounds
    wc, wl, off = c1 - c0, hi - lo, c0 - lo
    row_id = lax.broadcasted_iota(jnp.int32, (wc, C), 0)
    left = pltpu.roll(v, 1, 0)[off : off + wc]
    right = pltpu.roll(v, wl - 1, 0)[off : off + wc]
    if c0 == 0:
        left = jnp.where(row_id == 0, 0.0, left)
    if c1 == W:
        right = jnp.where(row_id == wc - 1, 0.0, right)
    dst[rows, 0:C] = left.astype(BF16)
    dst[rows, C : 2 * C] = v[off : off + wc].astype(BF16)
    dst[rows, 2 * C : 3 * C] = right.astype(BF16)


def gate_into(mixed, gated, at, total, gain):
    one = total.astype(BF16)
    normed = rms(one.astype(F32), gain)
    mixed[at] = one
    gated[at] = (normed / (1.0 + jnp.exp(-normed))).astype(BF16)


def edge_kernel(info, own, sib, same, cross, g1, g2, w, mixed, gated, info_out, wv, x, sems):
    k = info[0]
    copies = [
        pltpu.make_async_copy(w.at[tap], wv.at[role], sems.at[role])
        for role, tap in enumerate((1, 2 - 2 * k, 2 * k))
    ]
    for copy in copies:
        copy.start()
    pass_on(info, info_out)
    gain = g1[...]
    gain_halo = gain * info[2].astype(F32)
    bounds = (0, W, 0, W)
    for slot in range(2):
        for role in range(3):
            for i in range(EDGE):
                if role < 2:
                    v = (own, sib)[slot][MAIN + i, k if role == 0 else 1 - k]
                else:
                    v = (same, cross)[slot][i]
                v = rms(v.astype(F32), gain_halo if role == 2 else gain)
                shifted_into(x.at[slot, role], slice(i * W, (i + 1) * W), v, bounds)
    for slot in range(2):
        total = (own, sib)[slot][MAIN:8, k].astype(F32).reshape(EDGE * W, C)
        for role in range(3):
            if slot == 0:
                copies[role].wait()
            total = total + mm(x[slot, role], wv[role])
        at = pl.ds(EDGE * (k if slot == 0 else 1 - k), EDGE)
        gate_into(mixed, gated, at, total.reshape(EDGE, W, C), g2[...])


def edge_stage(info, own, sib, same, cross, g1, g2, w):
    shape = jax.ShapeDtypeStruct((2 * EDGE, W, C), BF16)
    return pl.pallas_call(
        edge_kernel,
        out_shape=(shape, shape, INFO, jax.ShapeDtypeStruct((3, 3 * C, C), BF16)),
        in_specs=[SMEM] + [VMEM] * 6 + [HBM],
        out_specs=(VMEM, VMEM, SMEM, VMEM),
        scratch_shapes=[
            pltpu.VMEM((2, 3, EDGE * W, 3 * C), BF16),
            pltpu.SemaphoreType.DMA((3,)),
        ],
        compiler_params=pltpu.CompilerParams(vmem_limit_bytes=24 * 2**20),
        cost_estimate=pl.CostEstimate(
            flops=2 * 4 * W * 9 * C * C, bytes_accessed=9 * C * C * 2, transcendentals=0
        ),
        name="edge",
    )(info, own, sib, same, cross, g1, g2, w)


def inner_kernel(j, info, own, sib, g1, wv, partial, info_out, x):
    pass_on(info, info_out)
    bounds = window(j)
    c0, c1, lo, hi = bounds
    wc = c1 - c0
    k = info[0]
    gain = g1[...]
    step = frames_per_step(MAIN, wc, 256)

    def prepare(index, role):
        for i in range(step):
            slot, at = divmod(index * step + i, MAIN)
            v = (own, sib)[slot][at, k if role == 0 else 1 - k, lo:hi, :].astype(F32)
            shifted_into(x.at[index % 2, role], slice(i * wc, (i + 1) * wc), rms(v, gain), bounds)

    for role in range(2):
        prepare(0, role)
    for index in range(2 * MAIN // step):
        slot, at = divmod(index * step, MAIN)
        acc = (own, sib)[slot][at : at + step, k, c0:c1, :].astype(F32).reshape(step * wc, C)
        for role in range(2):
            acc = acc + mm(x[index % 2, role], wv[role])
            if index + 1 < 2 * MAIN // step:
                prepare(index + 1, role)
        partial[index * step : (index + 1) * step] = acc.reshape(step, wc, C)


def inner_stage(j, info, own, sib, g1, wv):
    c0, c1, _, _ = window(j)
    wc = c1 - c0
    return pl.pallas_call(
        functools.partial(inner_kernel, j),
        out_shape=(jax.ShapeDtypeStruct((2 * MAIN, wc, C), F32), INFO),
        in_specs=[SMEM, VMEM, VMEM, VMEM, VMEM],
        out_specs=(VMEM, SMEM),
        scratch_shapes=[pltpu.VMEM((2, 2, frames_per_step(MAIN, wc, 256) * wc, 3 * C), BF16)],
        compiler_params=pltpu.CompilerParams(vmem_limit_bytes=20 * 2**20),
        cost_estimate=pl.CostEstimate(
            flops=2 * 12 * wc * 6 * C * C, bytes_accessed=6 * C * C * 2, transcendentals=0
        ),
        name=f"inner_{j}",
    )(info, own, sib, g1, wv)


def halo_kernel(j, n_pieces, info, partial, *refs):
    same = refs[:n_pieces]
    cross = refs[n_pieces : 2 * n_pieces]
    g1, g2, wv, mixed, gated, info_out, x = refs[2 * n_pieces :]
    pass_on(info, info_out)
    bounds = window(j)
    c0, c1, lo, hi = bounds
    wc = c1 - c0
    k = info[0]
    first = j + 1 - n_pieces
    gain_one = g1[...] * info[2].astype(F32)
    gain_two = g2[...]
    step = frames_per_step(MAIN, wc, 256)

    def prepare(index):
        for i in range(step):
            slot, at = divmod(index * step + i, MAIN)
            found = []
            for n in range(n_pieces):
                p0, p1 = piece_bounds(first + n)
                begin, end = max(p0, lo), min(p1, hi)
                found.append((same, cross)[slot][n][at, begin - p0 : end - p0, :].astype(F32))
            v = found[0] if n_pieces == 1 else jnp.concatenate(found, axis=0)
            shifted_into(x.at[index % 2], slice(i * wc, (i + 1) * wc), rms(v, gain_one), bounds)

    def finish(index, total):
        slot, at = divmod(index * step, MAIN)
        to = pl.ds(at + MAIN * (k if slot == 0 else 1 - k), step)
        gate_into(mixed, gated, to, total.reshape(step, wc, C), gain_two)

    prepare(0)
    last = None
    for index in range(2 * MAIN // step):
        total = partial[index * step : (index + 1) * step].reshape(step * wc, C)
        total = total + mm(x[index % 2], wv[2])
        if last is not None:
            finish(index - 1, last)
        if index + 1 < 2 * MAIN // step:
            prepare(index + 1)
        last = total
    finish(2 * MAIN // step - 1, last)


def halo_stage(j, info, partial, same, cross, g1, g2, wv):
    c0, c1, _, _ = window(j)
    wc = c1 - c0
    first = max(0, j - 1)
    same, cross = same[first : j + 1], cross[first : j + 1]
    n = len(same)
    shape = jax.ShapeDtypeStruct((2 * MAIN, wc, C), BF16)
    return pl.pallas_call(
        functools.partial(halo_kernel, j, n),
        out_shape=(shape, shape, INFO),
        in_specs=[SMEM] + [VMEM] * (2 * n + 4),
        out_specs=(VMEM, VMEM, SMEM),
        scratch_shapes=[pltpu.VMEM((2, frames_per_step(MAIN, wc, 256) * wc, 3 * C), BF16)],
        compiler_params=pltpu.CompilerParams(vmem_limit_bytes=18 * 2**20),
        cost_estimate=pl.CostEstimate(
            flops=2 * 12 * wc * 3 * C * C, bytes_accessed=3 * C * C * 2, transcendentals=0
        ),
        name=f"halo_{j}",
    )(info, partial, *same, *cross, g1, g2, wv)


def place_of(f):
    core, at = divmod(f, 8)
    return (1, core * EDGE + at - MAIN) if at >= MAIN else (0, core * MAIN + at)


def temporal_kernel(j, info, gated, edge_gated, before, mixed, edge_mixed, w, g3, *refs):
    mixed_two, n_first, n_rest, info_out, x = refs
    pass_on(info, info_out)
    c0, c1 = CUTS[j], CUTS[j + 1]
    wc = c1 - c0
    seen = before[:, c0:c1, :].reshape(2 * wc, C)
    x[0 : 2 * wc] = jnp.where(info[1] > 0, seen, jnp.zeros_like(seen))

    def frame(main, edge, f):
        which, at = place_of(f)
        return edge[at, c0:c1, :] if which else main[at]

    for f in range(NF):
        x[(f + 2) * wc : (f + 3) * wc] = frame(gated, edge_gated, f)
    gain = g3[...]
    step = frames_per_step(NF, wc, 256)
    for f0 in range(0, NF, step):
        acc = sum(
            mm(x[(f0 + tap) * wc : (f0 + tap + step) * wc, :], w[tap]) for tap in range(3)
        )
        for i in range(step):
            f = f0 + i
            base = frame(mixed, edge_mixed, f).astype(F32)
            two = (acc[i * wc : (i + 1) * wc] + base).astype(BF16)
            mixed_two[f] = two
            normed = rms(two.astype(F32), gain).astype(BF16)
            if f == 0:
                n_first[0] = normed
            else:
                n_rest[f - 1] = normed


def temporal_stage(j, info, gated, edge_gated, before, mixed, edge_mixed, w, g3):
    wc = CUTS[j + 1] - CUTS[j]
    return pl.pallas_call(
        functools.partial(temporal_kernel, j),
        out_shape=(
            jax.ShapeDtypeStruct((NF, wc, C), BF16),
            jax.ShapeDtypeStruct((1, wc, C), BF16),
            jax.ShapeDtypeStruct((NF - 1, wc, C), BF16),
            INFO,
        ),
        in_specs=[SMEM] + [VMEM] * 7,
        out_specs=(VMEM, VMEM, VMEM, SMEM),
        scratch_shapes=[pltpu.VMEM(((NF + 2) * wc, C), BF16)],
        compiler_params=pltpu.CompilerParams(vmem_limit_bytes=16 * 2**20),
        cost_estimate=pl.CostEstimate(
            flops=2 * NF * wc * 3 * C * C, bytes_accessed=3 * C * C * 2, transcendentals=0
        ),
        name=f"temporal_{j}",
    )(info, gated, edge_gated, before, mixed, edge_mixed, w, g3)


def grouped_store(dst, frame, product, wc):
    for g in range(wc // 8):
        pair = jnp.concatenate(
            [product[g * 8 : g * 8 + 8], product[wc + g * 8 : wc + g * 8 + 8]], axis=0
        )
        dst[g, frame * 8 : frame * 8 + 16, :] = pair.astype(BF16)


def qkv_kernel(wc, info, n_first, n_rest, wq, wk, wv, q, k, v, info_out, x):
    pass_on(info, info_out)
    x[0:wc] = n_first[0]
    x[wc:] = n_rest[...].reshape((NF - 1) * wc, C)
    for f0 in range(0, NF, 4):
        rows = x[f0 * wc : (f0 + 4) * wc, :]
        for w, dst, scale in ((wq, q, 0.125), (wk, k, None), (wv, v, None)):
            product = mm(rows, w[...])
            if scale is not None:
                product = product * scale
            grouped_store(dst, f0, product[: 2 * wc], wc)
            grouped_store(dst, f0 + 2, product[2 * wc :], wc)


def qkv_stage(j, info, n_first, n_rest, wq, wk, wv):
    wc = CUTS[j + 1] - CUTS[j]
    shape = jax.ShapeDtypeStruct((wc // 8, NF * 8, C), BF16)
    return pl.pallas_call(
        functools.partial(qkv_kernel, wc),
        out_shape=(shape, shape, shape, INFO),
        in_specs=[SMEM] + [VMEM] * 5,
        out_specs=(VMEM, VMEM, VMEM, SMEM),
        scratch_shapes=[pltpu.VMEM((NF * wc, C), BF16)],
        compiler_params=pltpu.CompilerParams(vmem_limit_bytes=20 * 2**20),
        cost_estimate=pl.CostEstimate(
            flops=2 * NF * wc * 3 * C * C, bytes_accessed=3 * C * C * 2, transcendentals=0
        ),
        name=f"project_{j}",
    )(info, n_first, n_rest, wq, wk, wv)


def attend_kernel(wc, info, ctx, wk, wv, wo, q, k, v, mixed_two, *refs):
    blocks, (info_out, x, kc, vc, att, out) = refs[:8], refs[8:]
    pass_on(info, info_out)
    groups = wc // 8
    rows = NF * 8
    x[0:wc] = jnp.zeros((wc, C), BF16)
    x[wc:] = ctx[...].reshape((NF - 1) * wc, C)
    for f0 in range(0, NF, 4):
        part = x[f0 * wc : (f0 + 4) * wc, :]
        for w, dst in ((wk, kc), (wv, vc)):
            product = mm(part, w[...])
            grouped_store(dst, f0, product[: 2 * wc], wc)
            grouped_store(dst, f0 + 2, product[2 * wc :], wc)
    row = lax.broadcasted_iota(jnp.int32, (rows, 2 * rows), 0)
    key = lax.broadcasted_iota(jnp.int32, (rows, 2 * rows), 1)
    lag = row // 8 + NF - key // 8
    allowed = (row % 8 == key % 8) & (lag >= 0) & (lag < NF)
    allowed = allowed & ((key >= rows) | (info[1] > 0))
    bias = jnp.where(allowed, 0.0, -1e30).astype(F32)
    lane_head = lax.broadcasted_iota(jnp.int32, (rows, 4 * HD), 1) // HD
    for g in range(groups):
        for half in range(2):
            lanes = slice(half * 4 * HD, (half + 1) * 4 * HD)
            keys = jnp.concatenate([kc[g, :, lanes], k[g, :, lanes]], axis=0)
            values = jnp.concatenate([vc[g, :, lanes], v[g, :, lanes]], axis=0)
            queries = q[g, :, lanes]
            stacked = jnp.concatenate(
                [jnp.where(lane_head == h, queries, jnp.zeros_like(queries)) for h in range(4)],
                axis=0,
            )
            score = lax.dot_general(
                stacked, keys, (((1,), (1,)), ((), ())), preferred_element_type=F32
            )
            score = score.reshape(4, rows, 2 * rows) + bias[None]
            e = jnp.exp(score - jnp.max(score, axis=-1, keepdims=True))
            scales = 1.0 / jnp.sum(e, axis=-1, keepdims=True)
            got = mm(e.astype(BF16).reshape(4 * rows, 2 * rows), values)
            total, scale = got[:rows], jnp.broadcast_to(scales[0], (rows, 4 * HD))
            for h in range(1, 4):
                total = jnp.where(lane_head == h, got[h * rows : (h + 1) * rows], total)
                scale = jnp.where(lane_head == h, scales[h], scale)
            total = total * scale
            att[g, :, lanes] = total.astype(BF16)
    for g in range(0, groups, 2):
        pair = att[g : g + 2].reshape(2 * rows, C)
        product = mm(pair, wo[...])
        for f in range(NF):
            piece = jnp.concatenate(
                [product[f * 8 : f * 8 + 8], product[rows + f * 8 : rows + f * 8 + 8]], axis=0
            )
            cols = slice(g * 8, g * 8 + 16)
            out[f, cols, :] = (piece + mixed_two[f, cols, :].astype(F32)).astype(BF16)
    core, band = info[0], info[3]
    for n in range(8):
        to_core = core if n < 4 else 1 - core
        blocks[n][...] = out[pl.ds(8 * to_core + 2 * lax.rem(band + n, 4), 2)]


def attend_stage(j, info, ctx, wk, wv, wo, q, k, v, mixed_two):
    wc = CUTS[j + 1] - CUTS[j]
    groups = wc // 8
    return pl.pallas_call(
        functools.partial(attend_kernel, wc),
        out_shape=(jax.ShapeDtypeStruct((2, wc, C), BF16),) * 8 + (INFO,),
        in_specs=[SMEM] + [VMEM] * 8,
        out_specs=(VMEM,) * 8 + (SMEM,),
        scratch_shapes=[
            pltpu.VMEM((NF * wc, C), BF16),
            pltpu.VMEM((groups, NF * 8, C), BF16),
            pltpu.VMEM((groups, NF * 8, C), BF16),
            pltpu.VMEM((groups, NF * 8, C), BF16),
            pltpu.VMEM((NF, wc, C), BF16),
        ],
        compiler_params=pltpu.CompilerParams(vmem_limit_bytes=20 * 2**20),
        cost_estimate=pl.CostEstimate(
            flops=2 * NF * wc * 7 * C * C, bytes_accessed=3 * C * C * 2, transcendentals=0
        ),
        name=f"attend_{j}",
    )(info, ctx, wk, wv, wo, q, k, v, mixed_two)


def place_kernel(j, info, *refs):
    blocks, (out, info_out, sems) = refs[:8], refs[-3:]
    pass_on(info, info_out)
    c0, c1 = CUTS[j], CUTS[j + 1]
    core, band = info[0], info[3]
    copies = []
    for n in range(8):
        from_core = core if n < 4 else 1 - core
        row = 2 * lax.rem(band + 8 - n, 4) + from_core
        copies.append(
            pltpu.make_async_copy(blocks[n], out.at[:, row, c0:c1, :], sems.at[n])
        )
    for copy in copies:
        copy.start()
    for copy in copies:
        copy.wait()


def place_stage(j, info, blocks, whole):
    earlier = () if whole is None else (whole,)
    return pl.pallas_call(
        functools.partial(place_kernel, j),
        out_shape=(jax.ShapeDtypeStruct((2, 8, W, C), BF16), INFO),
        in_specs=[SMEM] + [VMEM] * 8 + [HBM] * len(earlier),
        out_specs=(HBM, SMEM),
        scratch_shapes=[pltpu.SemaphoreType.DMA((8,))],
        input_output_aliases={9: 0} if earlier else {},
        compiler_params=pltpu.CompilerParams(vmem_limit_bytes=8 * 2**20),
        cost_estimate=pl.CostEstimate(flops=0, bytes_accessed=2**21, transcendentals=0),
        name=f"place_{j}",
    )(info, *blocks, *earlier)


def shards(
    latents,
    gain_one,
    spatial_weight,
    gain_two,
    temporal_weight,
    gain_three,
    query_weight,
    key_weight,
    value_weight,
    out_weight,
):
    index = lax.axis_index("frames")
    row = lax.axis_index("rows")
    k = index % 2
    halo_is_inside = jnp.where(k == 0, row > 0, row < lax.axis_size("rows") - 1)
    info = jnp.stack([k, index // 2, halo_is_inside.astype(jnp.int32), row]).astype(jnp.int32)
    g1, g2, g3 = (g.reshape(1, C) for g in (gain_one, gain_two, gain_three))
    w1 = spatial_weight.reshape(3, 3 * C, C)
    parts = range(len(CUTS) - 1)

    def rows_to(frames, columns, which, route, token):
        source = latents if token is None else lax.optimization_barrier((latents, token))[0]
        size = (frames[1] - frames[0], 1, columns[1] - columns[0], C)
        rows = lax.dynamic_slice(source, (frames[0], which, columns[0], 0), size)[:, 0]
        return routed(rows, route), rows

    edge_same, token = rows_to((MAIN, 8), (0, W), 1 - k, to_same_core, None)
    edge_cross, token = rows_to((MAIN, 8), (0, W), k, to_other_core, token)
    sib = routed(latents, to_sibling)
    same, cross = [], []
    for j in parts:
        for group, which, route in ((same, 1 - k, to_same_core), (cross, k, to_other_core)):
            got, token = rows_to((0, MAIN), piece_bounds(j), which, route, token)
            group.append(got)

    state = [{} for _ in parts]
    shared = {}

    def edge(j, info):
        shared["mixed"], shared["gated"], info, shared["w"] = edge_stage(
            info, latents, sib, edge_same, edge_cross, g1, g2, w1
        )
        shared["before"] = routed(shared["gated"][EDGE:], to_next_chip)
        return info

    def inside(j, info):
        state[j]["partial"], info = inner_stage(j, info, latents, sib, g1, shared["w"])
        return info

    def spatial(j, info):
        s = state[j]
        s["mixed"], s["gated"], info = halo_stage(
            j, info, s["partial"], same, cross, g1, g2, shared["w"]
        )
        return info

    def temporal(j, info):
        s = state[j]
        s["mixed"], s["first"], s["rest"], info = temporal_stage(
            j,
            info,
            s["gated"],
            shared["gated"],
            shared["before"],
            s["mixed"],
            shared["mixed"],
            temporal_weight,
            g3,
        )
        s["ctx"] = routed(s["rest"], to_next_chip)
        return info

    def project(j, info):
        s = state[j]
        s["q"], s["k"], s["v"], info = qkv_stage(
            j, info, s["first"], s["rest"], query_weight, key_weight, value_weight
        )
        return info

    def attend(j, info):
        s = state[j]
        *blocks, info = attend_stage(
            j,
            info,
            s["ctx"],
            key_weight,
            value_weight,
            out_weight,
            s["q"],
            s["k"],
            s["v"],
            s["mixed"],
        )
        for n in range(1, 8):
            blocks[n] = routed(blocks[n], lambda f, r: (f ^ (n // 4), r + n))
        s["blocks"] = blocks
        return info

    def place(j, info):
        shared["out"], info = place_stage(j, info, state[j]["blocks"], shared.get("out"))
        return info

    stages = {
        "e": edge,
        "i": inside,
        "s": spatial,
        "t": temporal,
        "p": project,
        "a": attend,
        "w": place,
    }
    for step in ORDER:
        info = stages[step[0]](int(step[1]), info)
    return shared["out"].reshape(-1, C)


def solution(mesh):
    placed = (P("frames", "rows", None, None),) + (P(),) * 9
    return jax.shard_map(
        shards, mesh=mesh, in_specs=placed, out_specs=P(("frames", "rows"), None), check_vma=False
    )
```

profile of v0, /device:TPU:1, one launch (start us, length us, event | category | flops | bytes accessed | tf_op | source)
XLA Modules:
  0.0 115.2 jit_solution(13085892273349261758)
XLA Ops:
  3.1 2.9 %collective-permute-start.1 = (bf16[2,128,512]{2,1,0:T(8,128)(2,1)}, bf16[2,128,512]{2,1,0:T(8,128)(2,1)S(1)}, u32[]{:S(2)}, u32[]{:S(2)}) collective-permute-start(bf16[2,128,512]{2,1,0:T(8,128)(2,1)} %dynamic-slice_bitcast_fusion.5), channel_id=1, source_target_pairs={{0,1},{1,2},{2,3},{3,0},{4,7},{5,4},{6,5},{7,6},{8,9},{9,10},{10,1... | collective-permute-start | bytes 786440 | tf_op jit(solution)/shard_map/ppermute | solution.py:35
  15.3 2.3 %copy-done.1 = bf16[3,3,512,512]{3,2,1,0:T(8,128)(2,1)S(1)} copy-done((bf16[3,3,512,512]{3,2,1,0:T(8,128)(2,1)S(1)}, bf16[3,3,512,512]{3,2,1,0:T(8,128)(2,1)}, u32[]{:S(2)}) %copy-start.1) | copy-done | bytes 4718616
  17.7 6.6 %edge.1 = (bf16[4,128,512]{2,1,0:T(8,128)(2,1)S(1)}, bf16[4,128,512]{2,1,0:T(8,128)(2,1)S(1)}, s32[4]{0:T(128)S(1)}, bf16[3,1536,512]{2,1,0:T(8,128)(2,1)S(1)}) custom-call(s32[4]{0:T(128)S(1)} %pad_add_fusion.info, bf16[8,2,128,512]{3,2,1,0:T(8,128)(2,1)S(1)} %copy-done, bf16[8,2,128,512]{3,2,1,0:T(8,128)(2,1)} %collective-permute-done.sib, ...), custom_call_target="tpu_custom_call" | custom-call | flops 2415919104 | bytes 4718592 | tf_op jit(solution)/shard_map/edge/pallas_call | solution.py:144
  25.5 4.7 %inner_0.1 = (f32[12,64,512]{2,1,0:T(8,128)S(1)}, s32[4]{0:T(128)S(1)}) custom-call(s32[4]{0:T(128)S(1)} %get-tuple-element.62.info, bf16[8,2,128,512]{3,2,1,0:T(8,128)(2,1)S(1)} %copy-done, bf16[8,2,128,512]{3,2,1,0:T(8,128)(2,1)} %collective-permute-done.sib, f32[1,512]{1,0:T(1,128)S(1)} %bitcast.23, ...), custom_call_target="tpu_custom_call" | custom-call | flops 2415919104 | bytes 3145728 | tf_op jit(solution)/shard_map/inner_0/pallas_call | solution.py:191
  30.3 2.7 %halo_0.1 = (bf16[12,64,512]{2,1,0:T(8,128)(2,1)S(1)}, bf16[12,64,512]{2,1,0:T(8,128)(2,1)S(1)}, s32[4]{0:T(128)S(1)}) custom-call(s32[4]{0:T(128)S(1)} %get-tuple-element.64.info, f32[12,64,512]{2,1,0:T(8,128)S(1)} %get-tuple-element.65.partial, bf16[6,72,512]{2,1,0:T(8,128)(2,1)S(1)} %collective-permute-done.3.refs_0_, ...), custom_call_target="tpu_custom_call" | custom-call | flops 1207959552 | bytes 1572864 | tf_op jit(solution)/shard_map/halo_0/pallas_call | solution.py:255
  33.0 3.1 %collective-permute-done.5.before = bf16[2,128,512]{2,1,0:T(8,128)(2,1)S(1)} collective-permute-done((bf16[2,128,512]{2,1,0:T(8,128)(2,1)S(1)}, bf16[2,128,512]{2,1,0:T(8,128)(2,1)S(1)}, u32[]{:S(2)}, u32[]{:S(2)}) %collective-permute-start.5) | collective-permute-done | bytes 262176 | tf_op jit(solution)/shard_map/ppermute | solution.py:35
  36.0 2.9 %temporal_0.1 = (bf16[16,64,512]{2,1,0:T(8,128)(2,1)S(1)}, bf16[1,64,512]{2,1,0:T(8,128)(2,1)S(1)}, bf16[15,64,512]{2,1,0:T(8,128)(2,1)S(1)}, s32[4]{0:T(128)S(1)}) custom-call(s32[4]{0:T(128)S(1)} %get-tuple-element.68.info, bf16[12,64,512]{2,1,0:T(8,128)(2,1)S(1)} %get-tuple-element.69.gated, bf16[4,128,512]{2,1,0:T(8,128)(2,1)S(1)} %get-tuple-element.70.edge_gated, ...), custom_call_target="tpu_custom_call" | custom-call | flops 1610612736 | bytes 1572864 | tf_op jit(solution)/shard_map/temporal_0/pallas_call | solution.py:308
  39.7 2.4 %collective-permute-start.6 = (bf16[6,56,512]{2,1,0:T(8,128)(2,1)S(1)}, bf16[6,56,512]{2,1,0:T(8,128)(2,1)S(1)}, u32[]{:S(2)}, u32[]{:S(2)}) collective-permute-start(bf16[6,56,512]{2,1,0:T(8,128)(2,1)S(1)} %copy-done.10), channel_id=1, source_target_pairs={{0,1},{1,2},{2,3},{3,0},{4,7},{5,4},{6,5},{7,6},{8,9},{9,10},{10,1... | collective-permute-start | bytes 1032200 | tf_op jit(solution)/shard_map/ppermute | solution.py:35
  42.0 4.7 %inner_1.1 = (f32[12,64,512]{2,1,0:T(8,128)S(1)}, s32[4]{0:T(128)S(1)}) custom-call(s32[4]{0:T(128)S(1)} %get-tuple-element.73.info, bf16[8,2,128,512]{3,2,1,0:T(8,128)(2,1)S(1)} %copy-done, bf16[8,2,128,512]{3,2,1,0:T(8,128)(2,1)} %collective-permute-done.sib, f32[1,512]{1,0:T(1,128)S(1)} %bitcast.25, ...), custom_call_target="tpu_custom_call" | custom-call | flops 2415919104 | bytes 3145728 | tf_op jit(solution)/shard_map/inner_1/pallas_call | solution.py:191
  46.7 3.0 %collective-permute-done.7.refs_3_ = bf16[6,56,512]{2,1,0:T(8,128)(2,1)S(1)} collective-permute-done((bf16[6,56,512]{2,1,0:T(8,128)(2,1)S(1)}, bf16[6,56,512]{2,1,0:T(8,128)(2,1)S(1)}, u32[]{:S(2)}, u32[]{:S(2)}) %collective-permute-start.7) | collective-permute-done | bytes 344096 | tf_op jit(solution)/shard_map/ppermute | solution.py:35
  49.7 2.7 %halo_1.1 = (bf16[12,64,512]{2,1,0:T(8,128)(2,1)S(1)}, bf16[12,64,512]{2,1,0:T(8,128)(2,1)S(1)}, s32[4]{0:T(128)S(1)}) custom-call(s32[4]{0:T(128)S(1)} %get-tuple-element.74.info, f32[12,64,512]{2,1,0:T(8,128)S(1)} %get-tuple-element.75.partial, bf16[6,72,512]{2,1,0:T(8,128)(2,1)S(1)} %collective-permute-done.3.refs_0_, ...), custom_call_target="tpu_custom_call" | custom-call | flops 1207959552 | bytes 1572864 | tf_op jit(solution)/shard_map/halo_1/pallas_call | solution.py:255
  52.5 3.0 %temporal_1.1 = (bf16[16,64,512]{2,1,0:T(8,128)(2,1)S(1)}, bf16[1,64,512]{2,1,0:T(8,128)(2,1)S(1)}, bf16[15,64,512]{2,1,0:T(8,128)(2,1)S(1)}, s32[4]{0:T(128)S(1)}) custom-call(s32[4]{0:T(128)S(1)} %get-tuple-element.78.info, bf16[12,64,512]{2,1,0:T(8,128)(2,1)S(1)} %get-tuple-element.79.gated, bf16[4,128,512]{2,1,0:T(8,128)(2,1)S(1)} %get-tuple-element.70.edge_gated, ...), custom_call_target="tpu_custom_call" | custom-call | flops 1610612736 | bytes 1572864 | tf_op jit(solution)/shard_map/temporal_1/pallas_call | solution.py:308
  55.8 2.8 %project_0.1 = (bf16[8,128,512]{2,1,0:T(8,128)(2,1)S(1)}, bf16[8,128,512]{2,1,0:T(8,128)(2,1)S(1)}, bf16[8,128,512]{2,1,0:T(8,128)(2,1)S(1)}, s32[4]{0:T(128)S(1)}) custom-call(s32[4]{0:T(128)S(1)} %get-tuple-element.81.info, bf16[1,64,512]{2,1,0:T(8,128)(2,1)S(1)} %get-tuple-element.82.n_first, bf16[15,64,512]{2,1,0:T(8,128)(2,1)S(1)} %get-tuple-element.83.n_rest, ...), custom_call_target="tpu_custom_call" | custom-call | flops 1610612736 | bytes 1572864 | tf_op jit(solution)/shard_map/project_0/pallas_call | solution.py:352
  58.7 2.8 %project_1.1 = (bf16[8,128,512]{2,1,0:T(8,128)(2,1)S(1)}, bf16[8,128,512]{2,1,0:T(8,128)(2,1)S(1)}, bf16[8,128,512]{2,1,0:T(8,128)(2,1)S(1)}, s32[4]{0:T(128)S(1)}) custom-call(s32[4]{0:T(128)S(1)} %get-tuple-element.84.info, bf16[1,64,512]{2,1,0:T(8,128)(2,1)S(1)} %get-tuple-element.85.n_first, bf16[15,64,512]{2,1,0:T(8,128)(2,1)S(1)} %get-tuple-element.86.n_rest, ...), custom_call_target="tpu_custom_call" | custom-call | flops 1610612736 | bytes 1572864 | tf_op jit(solution)/shard_map/project_1/pallas_call | solution.py:352
  61.5 4.5 %collective-permute-done.8.ctx = bf16[15,64,512]{2,1,0:T(8,128)(2,1)S(1)} collective-permute-done((bf16[15,64,512]{2,1,0:T(8,128)(2,1)S(1)}, bf16[15,64,512]{2,1,0:T(8,128)(2,1)S(1)}, u32[]{:S(2)}, u32[]{:S(2)}) %collective-permute-start.8) | collective-permute-done | bytes 983072 | tf_op jit(solution)/shard_map/ppermute | solution.py:35
  66.0 5.6 %attend_0.1 = (bf16[2,64,512]{2,1,0:T(8,128)(2,1)S(1)}, bf16[2,64,512]{2,1,0:T(8,128)(2,1)S(1)}, bf16[2,64,512]{2,1,0:T(8,128)(2,1)S(1)}, bf16[2,64,512]{2,1,0:T...) custom-call(s32[4]{0:T(128)S(1)} %get-tuple-element.87.info, ...), custom_call_target="tpu_custom_call" | custom-call | flops 3758096384 | bytes 1572864 | tf_op jit(solution)/shard_map/attend_0/pallas_call | solution.py:427
  73.7 2.6 %collective-permute-start.12 = (bf16[2,64,512]{2,1,0:T(8,128)(2,1)S(1)}, bf16[2,64,512]{2,1,0:T(8,128)(2,1)S(1)}, u32[]{:S(2)}, u32[]{:S(2)}) collective-permute-start(bf16[2,64,512]{2,1,0:T(8,128)(2,1)S(1)} %get-tuple-element.97), channel_id=1, source_target_pairs={{0,4},{1,5},{2,6},{3,7},{4,0},{5,1},{6,2},{7,3},{8,12},{9,13},{10,... | collective-permute-start | bytes 393224 | tf_op jit(solution)/shard_map/ppermute | solution.py:35
  77.3 4.0 %collective-permute-start.14 = (bf16[2,64,512]{2,1,0:T(8,128)(2,1)S(1)}, bf16[2,64,512]{2,1,0:T(8,128)(2,1)S(1)}, u32[]{:S(2)}, u32[]{:S(2)}) collective-permute-start(bf16[2,64,512]{2,1,0:T(8,128)(2,1)S(1)} %get-tuple-element.99), channel_id=1, source_target_pairs={{0,6},{1,7},{2,4},{3,5},{4,2},{5,3},{6,0},{7,1},{8,14},{9,15},{10,... | collective-permute-start | bytes 393224 | tf_op jit(solution)/shard_map/ppermute | solution.py:35
  81.3 2.2 %collective-permute-start.15 = (bf16[2,64,512]{2,1,0:T(8,128)(2,1)S(1)}, bf16[2,64,512]{2,1,0:T(8,128)(2,1)S(1)}, u32[]{:S(2)}, u32[]{:S(2)}) collective-permute-start(bf16[2,64,512]{2,1,0:T(8,128)(2,1)S(1)} %get-tuple-element.100), channel_id=1, source_target_pairs={{0,7},{1,4},{2,5},{3,6},{4,3},{5,0},{6,1},{7,2},{8,15},{9,12},{10,... | collective-permute-start | bytes 393224 | tf_op jit(solution)/shard_map/ppermute | solution.py:35
  85.2 2.3 %collective-permute-done.15.refs_7_ = bf16[2,64,512]{2,1,0:T(8,128)(2,1)S(1)} collective-permute-done((bf16[2,64,512]{2,1,0:T(8,128)(2,1)S(1)}, bf16[2,64,512]{2,1,0:T(8,128)(2,1)S(1)}, u32[]{:S(2)}, u32[]{:S(2)}) %collective-permute-start.15) | collective-permute-done | bytes 131104 | tf_op jit(solution)/shard_map/ppermute | solution.py:35
  87.5 2.2 %collective-permute-done.9.refs_1_ = bf16[2,64,512]{2,1,0:T(8,128)(2,1)S(1)} collective-permute-done((bf16[2,64,512]{2,1,0:T(8,128)(2,1)S(1)}, bf16[2,64,512]{2,1,0:T(8,128)(2,1)S(1)}, u32[]{:S(2)}, u32[]{:S(2)}) %collective-permute-start.9) | collective-permute-done | bytes 131104 | tf_op jit(solution)/shard_map/ppermute | solution.py:35
  91.9 5.6 %attend_1.1 = (bf16[2,64,512]{2,1,0:T(8,128)(2,1)S(1)}, bf16[2,64,512]{2,1,0:T(8,128)(2,1)S(1)}, bf16[2,64,512]{2,1,0:T(8,128)(2,1)S(1)}, bf16[2,64,512]{2,1,0:T...) custom-call(s32[4]{0:T(128)S(1)} %get-tuple-element.101.info, ...), custom_call_target="tpu_custom_call" | custom-call | flops 3758096384 | bytes 1572864 | tf_op jit(solution)/shard_map/attend_1/pallas_call | solution.py:427
  105.5 3.2 %collective-permute-start.23 = (bf16[2,64,512]{2,1,0:T(8,128)(2,1)S(1)}, bf16[2,64,512]{2,1,0:T(8,128)(2,1)S(1)}, u32[]{:S(2)}, u32[]{:S(2)}) collective-permute-start(bf16[2,64,512]{2,1,0:T(8,128)(2,1)S(1)} %get-tuple-element.114), channel_id=1, source_target_pairs={{0,7},{1,4},{2,5},{3,6},{4,3},{5,0},{6,1},{7,2},{8,15},{9,12},{10,... | collective-permute-start | bytes 393224 | tf_op jit(solution)/shard_map/ppermute | solution.py:35
  108.7 2.3 %collective-permute-done.21.refs_5_ = bf16[2,64,512]{2,1,0:T(8,128)(2,1)S(1)} collective-permute-done((bf16[2,64,512]{2,1,0:T(8,128)(2,1)S(1)}, bf16[2,64,512]{2,1,0:T(8,128)(2,1)S(1)}, u32[]{:S(2)}, u32[]{:S(2)}) %collective-permute-start.21) | collective-permute-done | bytes 131104 | tf_op jit(solution)/shard_map/ppermute | solution.py:35
  (67 shorter events, 33.6 us)
Async XLA Ops:
  0.0 15.3 %collective-permute-start = (bf16[8,2,128,512]{3,2,1,0:T(8,128)(2,1)}, bf16[8,2,128,512]{3,2,1,0:T(8,128)(2,1)}, u32[]{:S(2)}, u32[]{:S(2)}) collective-permute-start(bf16[8,2,128,512]{3,2,1,0:T(8,128)(2,1)} %own.5), channel_id=1, source_target_pairs={{0,4},{1,5},{2,6},{3,7},{4,0},{5,1},{6,2},{7,3},{8,12},{9,13},{10,... | collective-permute-start | bytes 6291464 | tf_op jit(solution)/shard_map/ppermute | solution.py:35
  3.1 12.2 %collective-permute-start.1 = (bf16[2,128,512]{2,1,0:T(8,128)(2,1)}, bf16[2,128,512]{2,1,0:T(8,128)(2,1)S(1)}, u32[]{:S(2)}, u32[]{:S(2)}) collective-permute-start(bf16[2,128,512]{2,1,0:T(8,128)(2,1)} %dynamic-slice_bitcast_fusion.5), channel_id=1, source_target_pairs={{0,1},{1,2},{2,3},{3,0},{4,7},{5,4},{6,5},{7,6},{8,9},{9,10},{10,1... | collective-permute-start | bytes 786440 | tf_op jit(solution)/shard_map/ppermute | solution.py:35
  7.7 7.6 %collective-permute-start.2 = (bf16[2,128,512]{2,1,0:T(8,128)(2,1)}, bf16[2,128,512]{2,1,0:T(8,128)(2,1)S(1)}, u32[]{:S(2)}, u32[]{:S(2)}) collective-permute-start(bf16[2,128,512]{2,1,0:T(8,128)(2,1)} %dynamic-slice_bitcast_fusion.4), channel_id=1, source_target_pairs={{0,7},{1,4},{2,5},{3,6},{4,1},{5,2},{6,3},{7,0},{8,15},{9,12},{10,... | collective-permute-start | bytes 786440 | tf_op jit(solution)/shard_map/ppermute | solution.py:35
  9.7 20.6 %collective-permute-start.3 = (bf16[6,72,512]{2,1,0:T(8,128)(2,1)}, bf16[6,72,512]{2,1,0:T(8,128)(2,1)S(1)}, u32[]{:S(2)}, u32[]{:S(2)}) collective-permute-start(bf16[6,72,512]{2,1,0:T(8,128)(2,1)} %dynamic-slice_bitcast_fusion.1), channel_id=1, source_target_pairs={{0,1},{1,2},{2,3},{3,0},{4,7},{5,4},{6,5},{7,6},{8,9},{9,10},{10,1... | collective-permute-start | bytes 1327112 | tf_op jit(solution)/shard_map/ppermute | solution.py:35
  12.9 17.4 %collective-permute-start.4 = (bf16[6,72,512]{2,1,0:T(8,128)(2,1)}, bf16[6,72,512]{2,1,0:T(8,128)(2,1)S(1)}, u32[]{:S(2)}, u32[]{:S(2)}) collective-permute-start(bf16[6,72,512]{2,1,0:T(8,128)(2,1)} %dynamic-slice_bitcast_fusion), channel_id=1, source_target_pairs={{0,7},{1,4},{2,5},{3,6},{4,1},{5,2},{6,3},{7,0},{8,15},{9,12},{10,... | collective-permute-start | bytes 1327112 | tf_op jit(solution)/shard_map/ppermute | solution.py:35
  24.3 11.8 %collective-permute-start.5 = (bf16[2,128,512]{2,1,0:T(8,128)(2,1)S(1)}, bf16[2,128,512]{2,1,0:T(8,128)(2,1)S(1)}, u32[]{:S(2)}, u32[]{:S(2)}) collective-permute-start(bf16[2,128,512]{2,1,0:T(8,128)(2,1)S(1)} %slice.3), channel_id=1, source_target_pairs={{0,8},{1,9},{2,10},{3,11},{4,12},{5,13},{6,14},{7,15},{8,16},{9,17... | collective-permute-start | bytes 786440 | tf_op jit(solution)/shard_map/ppermute | solution.py:35
  39.0 27.0 %collective-permute-start.8 = (bf16[15,64,512]{2,1,0:T(8,128)(2,1)S(1)}, bf16[15,64,512]{2,1,0:T(8,128)(2,1)S(1)}, u32[]{:S(2)}, u32[]{:S(2)}) collective-permute-start(bf16[15,64,512]{2,1,0:T(8,128)(2,1)S(1)} %get-tuple-element.83.n_rest), channel_id=1, source_target_pairs={{0,8},{1,9},{2,10},{3,11},{4,12},{5,13},{6,14},{7,15},{8,16},{9,17... | collective-permute-start | bytes 2949128 | tf_op jit(solution)/shard_map/ppermute | solution.py:35
  39.3 10.5 %collective-permute-start.7 = (bf16[6,56,512]{2,1,0:T(8,128)(2,1)S(1)}, bf16[6,56,512]{2,1,0:T(8,128)(2,1)S(1)}, u32[]{:S(2)}, u32[]{:S(2)}) collective-permute-start(bf16[6,56,512]{2,1,0:T(8,128)(2,1)S(1)} %dynamic-slice_bitcast_fusion.2), channel_id=1, source_target_pairs={{0,7},{1,4},{2,5},{3,6},{4,1},{5,2},{6,3},{7,0},{8,15},{9,12},{10,... | collective-permute-start | bytes 1032200 | tf_op jit(solution)/shard_map/ppermute | solution.py:35
  39.7 10.1 %collective-permute-start.6 = (bf16[6,56,512]{2,1,0:T(8,128)(2,1)S(1)}, bf16[6,56,512]{2,1,0:T(8,128)(2,1)S(1)}, u32[]{:S(2)}, u32[]{:S(2)}) collective-permute-start(bf16[6,56,512]{2,1,0:T(8,128)(2,1)S(1)} %copy-done.10), channel_id=1, source_target_pairs={{0,1},{1,2},{2,3},{3,0},{4,7},{5,4},{6,5},{7,6},{8,9},{9,10},{10,1... | collective-permute-start | bytes 1032200 | tf_op jit(solution)/shard_map/ppermute | solution.py:35
  55.5 36.4 %collective-permute-start.16 = (bf16[15,64,512]{2,1,0:T(8,128)(2,1)S(1)}, bf16[15,64,512]{2,1,0:T(8,128)(2,1)S(1)}, u32[]{:S(2)}, u32[]{:S(2)}) collective-permute-start(bf16[15,64,512]{2,1,0:T(8,128)(2,1)S(1)} %get-tuple-element.86.n_rest), channel_id=1, source_target_pairs={{0,8},{1,9},{2,10},{3,11},{4,12},{5,13},{6,14},{7,15},{8,16},{9,17... | collective-permute-start | bytes 2949128 | tf_op jit(solution)/shard_map/ppermute | solution.py:35
  71.6 5.7 %collective-permute-start.10 = (bf16[2,64,512]{2,1,0:T(8,128)(2,1)S(1)}, bf16[2,64,512]{2,1,0:T(8,128)(2,1)S(1)}, u32[]{:S(2)}, u32[]{:S(2)}) collective-permute-start(bf16[2,64,512]{2,1,0:T(8,128)(2,1)S(1)} %get-tuple-element.95), channel_id=1, source_target_pairs={{0,2},{1,3},{2,0},{3,1},{4,6},{5,7},{6,4},{7,5},{8,10},{9,11},{10,... | collective-permute-start | bytes 393224 | tf_op jit(solution)/shard_map/ppermute | solution.py:35
  73.4 7.9 %collective-permute-start.11 = (bf16[2,64,512]{2,1,0:T(8,128)(2,1)S(1)}, bf16[2,64,512]{2,1,0:T(8,128)(2,1)S(1)}, u32[]{:S(2)}, u32[]{:S(2)}) collective-permute-start(bf16[2,64,512]{2,1,0:T(8,128)(2,1)S(1)} %get-tuple-element.96), channel_id=1, source_target_pairs={{0,3},{1,0},{2,1},{3,2},{4,7},{5,4},{6,5},{7,6},{8,11},{9,8},{10,9... | collective-permute-start | bytes 393224 | tf_op jit(solution)/shard_map/ppermute | solution.py:35
  73.7 9.8 %collective-permute-start.12 = (bf16[2,64,512]{2,1,0:T(8,128)(2,1)S(1)}, bf16[2,64,512]{2,1,0:T(8,128)(2,1)S(1)}, u32[]{:S(2)}, u32[]{:S(2)}) collective-permute-start(bf16[2,64,512]{2,1,0:T(8,128)(2,1)S(1)} %get-tuple-element.97), channel_id=1, source_target_pairs={{0,4},{1,5},{2,6},{3,7},{4,0},{5,1},{6,2},{7,3},{8,12},{9,13},{10,... | collective-permute-start | bytes 393224 | tf_op jit(solution)/shard_map/ppermute | solution.py:35
  76.3 7.3 %collective-permute-start.13 = (bf16[2,64,512]{2,1,0:T(8,128)(2,1)S(1)}, bf16[2,64,512]{2,1,0:T(8,128)(2,1)S(1)}, u32[]{:S(2)}, u32[]{:S(2)}) collective-permute-start(bf16[2,64,512]{2,1,0:T(8,128)(2,1)S(1)} %get-tuple-element.98), channel_id=1, source_target_pairs={{0,5},{1,6},{2,7},{3,4},{4,1},{5,2},{6,3},{7,0},{8,13},{9,14},{10,... | collective-permute-start | bytes 393224 | tf_op jit(solution)/shard_map/ppermute | solution.py:35
  77.3 7.9 %collective-permute-start.14 = (bf16[2,64,512]{2,1,0:T(8,128)(2,1)S(1)}, bf16[2,64,512]{2,1,0:T(8,128)(2,1)S(1)}, u32[]{:S(2)}, u32[]{:S(2)}) collective-permute-start(bf16[2,64,512]{2,1,0:T(8,128)(2,1)S(1)} %get-tuple-element.99), channel_id=1, source_target_pairs={{0,6},{1,7},{2,4},{3,5},{4,2},{5,3},{6,0},{7,1},{8,14},{9,15},{10,... | collective-permute-start | bytes 393224 | tf_op jit(solution)/shard_map/ppermute | solution.py:35
  81.3 6.2 %collective-permute-start.15 = (bf16[2,64,512]{2,1,0:T(8,128)(2,1)S(1)}, bf16[2,64,512]{2,1,0:T(8,128)(2,1)S(1)}, u32[]{:S(2)}, u32[]{:S(2)}) collective-permute-start(bf16[2,64,512]{2,1,0:T(8,128)(2,1)S(1)} %get-tuple-element.100), channel_id=1, source_target_pairs={{0,7},{1,4},{2,5},{3,6},{4,3},{5,0},{6,1},{7,2},{8,15},{9,12},{10,... | collective-permute-start | bytes 393224 | tf_op jit(solution)/shard_map/ppermute | solution.py:35
  83.5 6.2 %collective-permute-start.9 = (bf16[2,64,512]{2,1,0:T(8,128)(2,1)S(1)}, bf16[2,64,512]{2,1,0:T(8,128)(2,1)S(1)}, u32[]{:S(2)}, u32[]{:S(2)}) collective-permute-start(bf16[2,64,512]{2,1,0:T(8,128)(2,1)S(1)} %get-tuple-element.94), channel_id=1, source_target_pairs={{0,1},{1,2},{2,3},{3,0},{4,5},{5,6},{6,7},{7,4},{8,9},{9,10},{10,1... | collective-permute-start | bytes 393224 | tf_op jit(solution)/shard_map/ppermute | solution.py:35
  97.5 6.8 %collective-permute-start.17 = (bf16[2,64,512]{2,1,0:T(8,128)(2,1)S(1)}, bf16[2,64,512]{2,1,0:T(8,128)(2,1)S(1)}, u32[]{:S(2)}, u32[]{:S(2)}) collective-permute-start(bf16[2,64,512]{2,1,0:T(8,128)(2,1)S(1)} %get-tuple-element.108), channel_id=1, source_target_pairs={{0,1},{1,2},{2,3},{3,0},{4,5},{5,6},{6,7},{7,4},{8,9},{9,10},{10,1... | collective-permute-start | bytes 393224 | tf_op jit(solution)/shard_map/ppermute | solution.py:35
  97.6 7.9 %collective-permute-start.18 = (bf16[2,64,512]{2,1,0:T(8,128)(2,1)S(1)}, bf16[2,64,512]{2,1,0:T(8,128)(2,1)S(1)}, u32[]{:S(2)}, u32[]{:S(2)}) collective-permute-start(bf16[2,64,512]{2,1,0:T(8,128)(2,1)S(1)} %get-tuple-element.109), channel_id=1, source_target_pairs={{0,2},{1,3},{2,0},{3,1},{4,6},{5,7},{6,4},{7,5},{8,10},{9,11},{10,... | collective-permute-start | bytes 393224 | tf_op jit(solution)/shard_map/ppermute | solution.py:35
  99.7 9.0 %collective-permute-start.19 = (bf16[2,64,512]{2,1,0:T(8,128)(2,1)S(1)}, bf16[2,64,512]{2,1,0:T(8,128)(2,1)S(1)}, u32[]{:S(2)}, u32[]{:S(2)}) collective-permute-start(bf16[2,64,512]{2,1,0:T(8,128)(2,1)S(1)} %get-tuple-element.110), channel_id=1, source_target_pairs={{0,3},{1,0},{2,1},{3,2},{4,7},{5,4},{6,5},{7,6},{8,11},{9,8},{10,9... | collective-permute-start | bytes 393224 | tf_op jit(solution)/shard_map/ppermute | solution.py:35
  100.2 8.5 %collective-permute-start.20 = (bf16[2,64,512]{2,1,0:T(8,128)(2,1)S(1)}, bf16[2,64,512]{2,1,0:T(8,128)(2,1)S(1)}, u32[]{:S(2)}, u32[]{:S(2)}) collective-permute-start(bf16[2,64,512]{2,1,0:T(8,128)(2,1)S(1)} %get-tuple-element.111), channel_id=1, source_target_pairs={{0,4},{1,5},{2,6},{3,7},{4,0},{5,1},{6,2},{7,3},{8,12},{9,13},{10,... | collective-permute-start | bytes 393224 | tf_op jit(solution)/shard_map/ppermute | solution.py:35
  101.3 9.7 %collective-permute-start.21 = (bf16[2,64,512]{2,1,0:T(8,128)(2,1)S(1)}, bf16[2,64,512]{2,1,0:T(8,128)(2,1)S(1)}, u32[]{:S(2)}, u32[]{:S(2)}) collective-permute-start(bf16[2,64,512]{2,1,0:T(8,128)(2,1)S(1)} %get-tuple-element.112), channel_id=1, source_target_pairs={{0,5},{1,6},{2,7},{3,4},{4,1},{5,2},{6,3},{7,0},{8,13},{9,14},{10,... | collective-permute-start | bytes 393224 | tf_op jit(solution)/shard_map/ppermute | solution.py:35
  104.3 6.8 %collective-permute-start.22 = (bf16[2,64,512]{2,1,0:T(8,128)(2,1)S(1)}, bf16[2,64,512]{2,1,0:T(8,128)(2,1)S(1)}, u32[]{:S(2)}, u32[]{:S(2)}) collective-permute-start(bf16[2,64,512]{2,1,0:T(8,128)(2,1)S(1)} %get-tuple-element.113), channel_id=1, source_target_pairs={{0,6},{1,7},{2,4},{3,5},{4,2},{5,3},{6,0},{7,1},{8,14},{9,15},{10,... | collective-permute-start | bytes 393224 | tf_op jit(solution)/shard_map/ppermute | solution.py:35
  105.5 7.4 %collective-permute-start.23 = (bf16[2,64,512]{2,1,0:T(8,128)(2,1)S(1)}, bf16[2,64,512]{2,1,0:T(8,128)(2,1)S(1)}, u32[]{:S(2)}, u32[]{:S(2)}) collective-permute-start(bf16[2,64,512]{2,1,0:T(8,128)(2,1)S(1)} %get-tuple-element.114), channel_id=1, source_target_pairs={{0,7},{1,4},{2,5},{3,6},{4,3},{5,0},{6,1},{7,2},{8,15},{9,12},{10,... | collective-permute-start | bytes 393224 | tf_op jit(solution)/shard_map/ppermute | solution.py:35
  (11 other events, 78.4 us)
where the time goes:
time: 116 us; the launch traced here: 115 us
  Pallas kernels  48.3 us (42%)
  starting transfers between devices  30.6 us (26%)
  waiting for transfers between devices  25.5 us (22%)
  local copies, waits for them, and re-layouts  10.2 us (9%)
    ppermute x24, starting transfers between devices, routed(): return lax.ppermute(x, AXES, pairs)  30.6 us
    ppermute x24, waiting for transfers between devices, routed(): return lax.ppermute(x, AXES, pairs)  25.5 us
    pallas_call x2, Pallas kernels, attend_stage(): pl.pallas_call(functools.partial(attend_kernel, wc), out_shape=(jax.Shape...  11.2 us
    pallas_call x2, Pallas kernels, inner_stage(): pl.pallas_call(functools.partial(inner_kernel, j), out_shape=(jax.ShapeDt...  9.4 us
    squeeze x6, local copies, waits for them, and re-layouts, rows_to(): lax.dynamic_slice(source, (frames[0], which, columns[0], 0), size)[:, 0]  7.75 us
    pallas_call x1, Pallas kernels, edge_stage(): pl.pallas_call(edge_kernel, out_shape=(shape, shape, INFO, jax.ShapeDtype...  6.56 us
    pallas_call x2, Pallas kernels, temporal_stage(): pl.pallas_call(functools.partial(temporal_kernel, j), out_shape=(jax.Shap...  5.91 us
    pallas_call x2, Pallas kernels, qkv_stage(): pl.pallas_call(functools.partial(qkv_kernel, wc), out_shape=(shape, shape...  5.63 us
  transfers between devices with their start and end apart: 24, of which 12 were waited for; matrix products, arithmetic and copies ran while one was open for 7% of the time, Pallas kernels for 33%

commit v1 on v0

--- a/solution.py
+++ b/solution.py
@@ -15,11 +15,12 @@
 RIM = 8
 EDGE = 2
 MAIN = 8 - EDGE
-CUTS = (0, 64, 128)
-ORDER = ("e0", "i0", "s0", "t0", "i1", "s1", "t1", "p0", "p1", "a0", "w0", "a1", "w1")
+CUTS = (0, 80, 128)
+ORDER = ("e0", "i0", "s0", "t0", "i1", "s1", "t1", "p0", "p1", "a0", "a1", "d0", "d1", "w0", "w1")
 AXES = ("frames", "rows")
 F32 = jnp.float32
 BF16 = jnp.bfloat16
+LIGHT = pl.CostEstimate(flops=0, bytes_accessed=0, transcendentals=0)
 HBM = pl.BlockSpec(memory_space=pltpu.HBM)
 SMEM = pl.BlockSpec(memory_space=pltpu.SMEM)
 VMEM = pl.BlockSpec(memory_space=pltpu.VMEM)
@@ -108,7 +109,29 @@
     gated[at] = (normed / (1.0 + jnp.exp(-normed))).astype(BF16)
 
 
-def edge_kernel(info, own, sib, same, cross, g1, g2, w, mixed, gated, info_out, wv, x, sems):
+def first_rows_kernel(info, latents, outer, inner, info_out):
+    pass_on(info, info_out)
+    k = info[0]
+    outer[...] = latents[MAIN:8, 1 - k]
+    inner[...] = latents[MAIN:8, k]
+
+
+def first_rows_stage(info, latents):
+    shape = jax.ShapeDtypeStruct((EDGE, W, C), BF16)
+    return pl.pallas_call(
+        first_rows_kernel,
+        out_shape=(shape, shape, INFO),
+        in_specs=[SMEM, VMEM],
+        out_specs=(VMEM, VMEM, SMEM),
+        compiler_params=pltpu.CompilerParams(vmem_limit_bytes=8 * 2**20),
+        cost_estimate=LIGHT,
+        name="first_rows",
+    )(info, latents)
+
+
+def other_rows_kernel(info, latents, w, *refs):
+    *pieces, wv, info_out, sems = refs
+    pass_on(info, info_out)
     k = info[0]
     copies = [
         pltpu.make_async_copy(w.at[tap], wv.at[role], sems.at[role])
@@ -116,6 +139,34 @@
     ]
     for copy in copies:
         copy.start()
+    for j in range(len(pieces) // 2):
+        p0, p1 = piece_bounds(j)
+        pieces[2 * j][...] = latents[0:MAIN, 1 - k, p0:p1, :]
+        pieces[2 * j + 1][...] = latents[0:MAIN, k, p0:p1, :]
+    for copy in copies:
+        copy.wait()
+
+
+def other_rows_stage(info, latents, w):
+    shapes = []
+    for j in range(len(CUTS) - 1):
+        p0, p1 = piece_bounds(j)
+        shapes += [jax.ShapeDtypeStruct((MAIN, p1 - p0, C), BF16)] * 2
+    shapes.append(jax.ShapeDtypeStruct((3, 3 * C, C), BF16))
+    return pl.pallas_call(
+        other_rows_kernel,
+        out_shape=shapes + [INFO],
+        in_specs=[SMEM, VMEM, HBM],
+        out_specs=[VMEM] * len(shapes) + [SMEM],
+        scratch_shapes=[pltpu.SemaphoreType.DMA((3,))],
+        compiler_params=pltpu.CompilerParams(vmem_limit_bytes=16 * 2**20),
+        cost_estimate=LIGHT,
+        name="other_rows",
+    )(info, latents, w)
+
+
+def edge_kernel(info, own, sib, same, cross, g1, g2, wv, mixed, gated, info_out, x):
+    k = info[0]
     pass_on(info, info_out)
     gain = g1[...]
     gain_halo = gain * info[2].astype(F32)
@@ -132,8 +183,6 @@
     for slot in range(2):
         total = (own, sib)[slot][MAIN:8, k].astype(F32).reshape(EDGE * W, C)
         for role in range(3):
-            if slot == 0:
-                copies[role].wait()
             total = total + mm(x[slot, role], wv[role])
         at = pl.ds(EDGE * (k if slot == 0 else 1 - k), EDGE)
         gate_into(mixed, gated, at, total.reshape(EDGE, W, C), g2[...])
@@ -143,17 +192,12 @@
     shape = jax.ShapeDtypeStruct((2 * EDGE, W, C), BF16)
     return pl.pallas_call(
         edge_kernel,
-        out_shape=(shape, shape, INFO, jax.ShapeDtypeStruct((3, 3 * C, C), BF16)),
-        in_specs=[SMEM] + [VMEM] * 6 + [HBM],
-        out_specs=(VMEM, VMEM, SMEM, VMEM),
-        scratch_shapes=[
-            pltpu.VMEM((2, 3, EDGE * W, 3 * C), BF16),
-            pltpu.SemaphoreType.DMA((3,)),
-        ],
+        out_shape=(shape, shape, INFO),
+        in_specs=[SMEM] + [VMEM] * 7,
+        out_specs=(VMEM, VMEM, SMEM),
+        scratch_shapes=[pltpu.VMEM((2, 3, EDGE * W, 3 * C), BF16)],
         compiler_params=pltpu.CompilerParams(vmem_limit_bytes=24 * 2**20),
-        cost_estimate=pl.CostEstimate(
-            flops=2 * 4 * W * 9 * C * C, bytes_accessed=9 * C * C * 2, transcendentals=0
-        ),
+        cost_estimate=LIGHT,
         name="edge",
     )(info, own, sib, same, cross, g1, g2, w)
 
@@ -165,7 +209,7 @@
     wc = c1 - c0
     k = info[0]
     gain = g1[...]
-    step = frames_per_step(MAIN, wc, 256)
+    step = frames_per_step(MAIN, wc, 300)
 
     def prepare(index, role):
         for i in range(step):
@@ -193,11 +237,9 @@
         out_shape=(jax.ShapeDtypeStruct((2 * MAIN, wc, C), F32), INFO),
         in_specs=[SMEM, VMEM, VMEM, VMEM, VMEM],
         out_specs=(VMEM, SMEM),
-        scratch_shapes=[pltpu.VMEM((2, 2, frames_per_step(MAIN, wc, 256) * wc, 3 * C), BF16)],
+        scratch_shapes=[pltpu.VMEM((2, 2, frames_per_step(MAIN, wc, 300) * wc, 3 * C), BF16)],
         compiler_params=pltpu.CompilerParams(vmem_limit_bytes=20 * 2**20),
-        cost_estimate=pl.CostEstimate(
-            flops=2 * 12 * wc * 6 * C * C, bytes_accessed=6 * C * C * 2, transcendentals=0
-        ),
+        cost_estimate=LIGHT,
         name=f"inner_{j}",
     )(info, own, sib, g1, wv)
 
@@ -214,7 +256,7 @@
     first = j + 1 - n_pieces
     gain_one = g1[...] * info[2].astype(F32)
     gain_two = g2[...]
-    step = frames_per_step(MAIN, wc, 256)
+    step = frames_per_step(MAIN, wc, 300)
 
     def prepare(index):
         for i in range(step):
@@ -257,11 +299,9 @@
         out_shape=(shape, shape, INFO),
         in_specs=[SMEM] + [VMEM] * (2 * n + 4),
         out_specs=(VMEM, VMEM, SMEM),
-        scratch_shapes=[pltpu.VMEM((2, frames_per_step(MAIN, wc, 256) * wc, 3 * C), BF16)],
+        scratch_shapes=[pltpu.VMEM((2, frames_per_step(MAIN, wc, 300) * wc, 3 * C), BF16)],
         compiler_params=pltpu.CompilerParams(vmem_limit_bytes=18 * 2**20),
-        cost_estimate=pl.CostEstimate(
-            flops=2 * 12 * wc * 3 * C * C, bytes_accessed=3 * C * C * 2, transcendentals=0
-        ),
+        cost_estimate=LIGHT,
         name=f"halo_{j}",
     )(info, partial, *same, *cross, g1, g2, wv)
 
@@ -286,7 +326,7 @@
     for f in range(NF):
         x[(f + 2) * wc : (f + 3) * wc] = frame(gated, edge_gated, f)
     gain = g3[...]
-    step = frames_per_step(NF, wc, 256)
+    step = frames_per_step(NF, wc, 320)
     for f0 in range(0, NF, step):
         acc = sum(
             mm(x[(f0 + tap) * wc : (f0 + tap + step) * wc, :], w[tap]) for tap in range(3)
@@ -317,9 +357,7 @@
         out_specs=(VMEM, VMEM, VMEM, SMEM),
         scratch_shapes=[pltpu.VMEM(((NF + 2) * wc, C), BF16)],
         compiler_params=pltpu.CompilerParams(vmem_limit_bytes=16 * 2**20),
-        cost_estimate=pl.CostEstimate(
-            flops=2 * NF * wc * 3 * C * C, bytes_accessed=3 * C * C * 2, transcendentals=0
-        ),
+        cost_estimate=LIGHT,
         name=f"temporal_{j}",
     )(info, gated, edge_gated, before, mixed, edge_mixed, w, g3)
 
@@ -356,15 +394,13 @@
         out_specs=(VMEM, VMEM, VMEM, SMEM),
         scratch_shapes=[pltpu.VMEM((NF * wc, C), BF16)],
         compiler_params=pltpu.CompilerParams(vmem_limit_bytes=20 * 2**20),
-        cost_estimate=pl.CostEstimate(
-            flops=2 * NF * wc * 3 * C * C, bytes_accessed=3 * C * C * 2, transcendentals=0
-        ),
+        cost_estimate=LIGHT,
         name=f"project_{j}",
     )(info, n_first, n_rest, wq, wk, wv)
 
 
 def attend_kernel(wc, info, ctx, wk, wv, wo, q, k, v, mixed_two, *refs):
-    blocks, (info_out, x, kc, vc, att, out) = refs[:8], refs[8:]
+    blocks, (info_out, x, kc, vc, att, out) = refs[:4], refs[4:]
     pass_on(info, info_out)
     groups = wc // 8
     rows = NF * 8
@@ -416,9 +452,10 @@
             cols = slice(g * 8, g * 8 + 16)
             out[f, cols, :] = (piece + mixed_two[f, cols, :].astype(F32)).astype(BF16)
     core, band = info[0], info[3]
-    for n in range(8):
-        to_core = core if n < 4 else 1 - core
-        blocks[n][...] = out[pl.ds(8 * to_core + 2 * lax.rem(band + n, 4), 2)]
+    for n in range(4):
+        at = 2 * lax.rem(band + n, 4)
+        blocks[n][0] = out[pl.ds(8 * core + at, 2)]
+        blocks[n][1] = out[pl.ds(8 - 8 * core + at, 2)]
 
 
 def attend_stage(j, info, ctx, wk, wv, wo, q, k, v, mixed_two):
@@ -426,9 +463,9 @@
     groups = wc // 8
     return pl.pallas_call(
         functools.partial(attend_kernel, wc),
-        out_shape=(jax.ShapeDtypeStruct((2, wc, C), BF16),) * 8 + (INFO,),
+        out_shape=(jax.ShapeDtypeStruct((2, 2, wc, C), BF16),) * 4 + (INFO,),
         in_specs=[SMEM] + [VMEM] * 8,
-        out_specs=(VMEM,) * 8 + (SMEM,),
+        out_specs=(VMEM,) * 4 + (SMEM,),
         scratch_shapes=[
             pltpu.VMEM((NF * wc, C), BF16),
             pltpu.VMEM((groups, NF * 8, C), BF16),
@@ -437,44 +474,61 @@
             pltpu.VMEM((NF, wc, C), BF16),
         ],
         compiler_params=pltpu.CompilerParams(vmem_limit_bytes=20 * 2**20),
-        cost_estimate=pl.CostEstimate(
-            flops=2 * NF * wc * 7 * C * C, bytes_accessed=3 * C * C * 2, transcendentals=0
-        ),
+        cost_estimate=LIGHT,
         name=f"attend_{j}",
     )(info, ctx, wk, wv, wo, q, k, v, mixed_two)
 
 
+def deal_kernel(info, *refs):
+    blocks, (give, info_out) = refs[:4], refs[4:]
+    pass_on(info, info_out)
+    for n in range(4):
+        give[n] = blocks[n][1]
+
+
+def deal_stage(j, info, blocks):
+    wc = CUTS[j + 1] - CUTS[j]
+    return pl.pallas_call(
+        deal_kernel,
+        out_shape=(jax.ShapeDtypeStruct((4, 2, wc, C), BF16), INFO),
+        in_specs=[SMEM] + [VMEM] * 4,
+        out_specs=(VMEM, SMEM),
+        compiler_params=pltpu.CompilerParams(vmem_limit_bytes=8 * 2**20),
+        cost_estimate=LIGHT,
+        name=f"deal_{j}",
+    )(info, *blocks)
+
+
 def place_kernel(j, info, *refs):
-    blocks, (out, info_out, sems) = refs[:8], refs[-3:]
+    blocks, got, (out, info_out, sems) = refs[:4], refs[4], refs[-3:]
     pass_on(info, info_out)
     c0, c1 = CUTS[j], CUTS[j + 1]
     core, band = info[0], info[3]
     copies = []
-    for n in range(8):
-        from_core = core if n < 4 else 1 - core
-        row = 2 * lax.rem(band + 8 - n, 4) + from_core
-        copies.append(
-            pltpu.make_async_copy(blocks[n], out.at[:, row, c0:c1, :], sems.at[n])
-        )
+    for n in range(4):
+        row = 2 * lax.rem(band + 4 - n, 4)
+        for i, (src, at) in enumerate(((blocks[n].at[0], core), (got.at[n], 1 - core))):
+            dst = out.at[:, row + at, c0:c1, :]
+            copies.append(pltpu.make_async_copy(src, dst, sems.at[2 * n + i]))
     for copy in copies:
         copy.start()
     for copy in copies:
         copy.wait()
 
 
-def place_stage(j, info, blocks, whole):
+def place_stage(j, info, blocks, got, whole):
     earlier = () if whole is None else (whole,)
     return pl.pallas_call(
         functools.partial(place_kernel, j),
         out_shape=(jax.ShapeDtypeStruct((2, 8, W, C), BF16), INFO),
-        in_specs=[SMEM] + [VMEM] * 8 + [HBM] * len(earlier),
+        in_specs=[SMEM] + [VMEM] * 5 + [HBM] * len(earlier),
         out_specs=(HBM, SMEM),
         scratch_shapes=[pltpu.SemaphoreType.DMA((8,))],
-        input_output_aliases={9: 0} if earlier else {},
+        input_output_aliases={6: 0} if earlier else {},
         compiler_params=pltpu.CompilerParams(vmem_limit_bytes=8 * 2**20),
-        cost_estimate=pl.CostEstimate(flops=0, bytes_accessed=2**21, transcendentals=0),
+        cost_estimate=LIGHT,
         name=f"place_{j}",
-    )(info, *blocks, *earlier)
+    )(info, *blocks, got, *earlier)
 
 
 def shards(
@@ -498,39 +552,33 @@
     w1 = spatial_weight.reshape(3, 3 * C, C)
     parts = range(len(CUTS) - 1)
 
-    def rows_to(frames, columns, which, route, token):
-        source = latents if token is None else lax.optimization_barrier((latents, token))[0]
-        size = (frames[1] - frames[0], 1, columns[1] - columns[0], C)
-        rows = lax.dynamic_slice(source, (frames[0], which, columns[0], 0), size)[:, 0]
-        return routed(rows, route), rows
-
-    edge_same, token = rows_to((MAIN, 8), (0, W), 1 - k, to_same_core, None)
-    edge_cross, token = rows_to((MAIN, 8), (0, W), k, to_other_core, token)
     sib = routed(latents, to_sibling)
-    same, cross = [], []
-    for j in parts:
-        for group, which, route in ((same, 1 - k, to_same_core), (cross, k, to_other_core)):
-            got, token = rows_to((0, MAIN), piece_bounds(j), which, route, token)
-            group.append(got)
+    outer, inner, info = first_rows_stage(info, latents)
+    edge_same, edge_cross = routed(outer, to_same_core), routed(inner, to_other_core)
+    *pieces, weights, info = other_rows_stage(info, latents, w1)
+    *pieces, edge_same, edge_cross = lax.optimization_barrier((*pieces, edge_same, edge_cross))
+    own = latents
+    same = [routed(piece, to_same_core) for piece in pieces[0::2]]
+    cross = [routed(piece, to_other_core) for piece in pieces[1::2]]
 
     state = [{} for _ in parts]
     shared = {}
 
     def edge(j, info):
-        shared["mixed"], shared["gated"], info, shared["w"] = edge_stage(
-            info, latents, sib, edge_same, edge_cross, g1, g2, w1
+        shared["mixed"], shared["gated"], info = edge_stage(
+            info, own, sib, edge_same, edge_cross, g1, g2, weights
         )
         shared["before"] = routed(shared["gated"][EDGE:], to_next_chip)
         return info
 
     def inside(j, info):
-        state[j]["partial"], info = inner_stage(j, info, latents, sib, g1, shared["w"])
+        state[j]["partial"], info = inner_stage(j, info, own, sib, g1, weights)
         return info
 
     def spatial(j, info):
         s = state[j]
         s["mixed"], s["gated"], info = halo_stage(
-            j, info, s["partial"], same, cross, g1, g2, shared["w"]
+            j, info, s["partial"], same, cross, g1, g2, weights
         )
         return info
 
@@ -571,13 +619,23 @@
             s["v"],
             s["mixed"],
         )
-        for n in range(1, 8):
-            blocks[n] = routed(blocks[n], lambda f, r: (f ^ (n // 4), r + n))
+        for n in (2, 1, 3):
+            blocks[n] = routed(blocks[n], lambda f, r: (f, r + n))
         s["blocks"] = blocks
         return info
 
+    def deal(j, info):
+        s = state[j]
+        give, info = deal_stage(j, info, s["blocks"])
+        if j + 1 < len(state):
+            later = state[j + 1]["blocks"]
+            give, *later[1:] = lax.optimization_barrier((give, *later[1:]))
+        s["got"] = routed(give, to_sibling)
+        return info
+
     def place(j, info):
-        shared["out"], info = place_stage(j, info, state[j]["blocks"], shared.get("out"))
+        s = state[j]
+        shared["out"], info = place_stage(j, info, s["blocks"], s["got"], shared.get("out"))
         return info
 
     stages = {
@@ -587,6 +645,7 @@
         "t": temporal,
         "p": project,
         "a": attend,
+        "d": deal,
         "w": place,
     }
     for step in ORDER:

time: 116 us -> 110 us (0.948)
  local copies, waits for them, and re-layouts: 10.2 us -> 3.99 us
  waiting for transfers between devices: 25.5 us -> 29 us
  starting transfers between devices: 30.6 us -> 27.7 us
    squeeze x6 -> x0, local copies, waits for them, and re-layouts: 7.75 us -> none  [rows_to(): lax.dynamic_slice(source, (frames[0], which, columns[0], 0), size)[:, 0]]
    ppermute x24 -> x18, waiting for transfers between devices: 25.5 us -> 29 us  [routed(): return lax.ppermute(x, AXES, pairs)]
    ppermute x24 -> x18, starting transfers between devices: 30.6 us -> 27.7 us  [routed(): return lax.ppermute(x, AXES, pairs)]
    pallas_call x1 -> x5, Pallas kernels: 6.56 us -> 9.24 us  [the longest x1 4.23 us: edge_stage(): pl.pallas_call(edge_kernel, out_shape=(shape, shape, INFO), in_specs=[SME...]
    pallas_call x2, Pallas kernels: 9.4 us -> 7.06 us  [inner_stage(): pl.pallas_call(functools.partial(inner_kernel, j), out_shape=(jax.ShapeDt...]
    unnamed x22, local copies, waits for them, and re-layouts: 2.38 us -> 3.97 us
  transfers between devices with their start and end apart: 24 -> 18, of which waited for: 12 -> 12; matrix products, arithmetic and copies ran while one was open for 7% -> 0% of each run, Pallas kernels for 33% -> 40%
where the time goes in v1:
time: 110 us
  Pallas kernels  48.8 us (44%)
  waiting for transfers between devices  29 us (26%)
  starting transfers between devices  27.7 us (25%)
  local copies, waits for them, and re-layouts  3.99 us (4%)
    ppermute x18, waiting for transfers between devices, routed(): return lax.ppermute(x, AXES, pairs)  29 us
    ppermute x18, starting transfers between devices, routed(): return lax.ppermute(x, AXES, pairs)  27.7 us
    pallas_call x2, Pallas kernels, attend_stage(): pl.pallas_call(functools.partial(attend_kernel, wc), out_shape=(jax.Shape...  11.5 us
    pallas_call x2, Pallas kernels, inner_stage(): pl.pallas_call(functools.partial(inner_kernel, j), out_shape=(jax.ShapeDt...  7.06 us
    pallas_call x2, Pallas kernels, temporal_stage(): pl.pallas_call(functools.partial(temporal_kernel, j), out_shape=(jax.Shap...  5.97 us
    pallas_call x2, Pallas kernels, halo_stage(): pl.pallas_call(functools.partial(halo_kernel, j, n), out_shape=(shape, sh...  5.61 us
    pallas_call x2, Pallas kernels, qkv_stage(): pl.pallas_call(functools.partial(qkv_kernel, wc), out_shape=(shape, shape...  5.22 us
    pallas_call x2, Pallas kernels, place_stage(): pl.pallas_call(functools.partial(place_kernel, j), out_shape=(jax.ShapeDt...  4.26 us
  transfers between devices with their start and end apart: 18, of which 12 were waited for; matrix products, arithmetic and copies ran while one was open for 0% of the time, Pallas kernels for 40%

profile of v1, /device:TPU:1, one launch (start us, length us, event | category | flops | bytes accessed | tf_op | source)
XLA Modules:
  0.0 110.0 jit_solution(18248429274454832542)
XLA Ops:
  4.2 2.9 %collective-permute-start.1 = (bf16[2,128,512]{2,1,0:T(8,128)(2,1)S(1)}, bf16[2,128,512]{2,1,0:T(8,128)(2,1)S(1)}, u32[]{:S(2)}, u32[]{:S(2)}) collective-permute-start(bf16[2,128,512]{2,1,0:T(8,128)(2,1)S(1)} %get-tuple-element.76), channel_id=1, source_target_pairs={{0,1},{1,2},{2,3},{3,0},{4,7},{5,4},{6,5},{7,6},{8,9},{9,10},{10,1... | collective-permute-start | bytes 786440 | tf_op jit(solution)/shard_map/ppermute | solution.py:36
  7.2 2.3 %copy-done.5 = bf16[3,3,512,512]{3,2,1,0:T(8,128)(2,1)S(1)} copy-done((bf16[3,3,512,512]{3,2,1,0:T(8,128)(2,1)S(1)}, bf16[3,3,512,512]{3,2,1,0:T(8,128)(2,1)}, u32[]{:S(2)}) %copy-start.5) | copy-done | bytes 4718616
  13.2 3.1 %collective-permute-start.3 = (bf16[6,88,512]{2,1,0:T(8,128)(2,1)S(1)}, bf16[6,88,512]{2,1,0:T(8,128)(2,1)S(1)}, u32[]{:S(2)}, u32[]{:S(2)}) collective-permute-start(bf16[6,88,512]{2,1,0:T(8,128)(2,1)S(1)} %get-tuple-element.84), channel_id=1, source_target_pairs={{0,1},{1,2},{2,3},{3,0},{4,7},{5,4},{6,5},{7,6},{8,9},{9,10},{10,1... | collective-permute-start | bytes 1622024 | tf_op jit(solution)/shard_map/ppermute | solution.py:36
  16.4 4.2 %edge.1 = (bf16[4,128,512]{2,1,0:T(8,128)(2,1)S(1)}, bf16[4,128,512]{2,1,0:T(8,128)(2,1)S(1)}, s32[4]{0:T(128)S(1)}) custom-call(s32[4]{0:T(128)S(1)} %get-tuple-element.71.info, bf16[8,2,128,512]{3,2,1,0:T(8,128)(2,1)S(1)} %copy-done.1, bf16[8,2,128,512]{3,2,1,0:T(8,128)(2,1)S(1)} %collective-permute-done.sib, ...), custom_call_target="tpu_custom_call" | custom-call | tf_op jit(solution)/shard_map/edge/pallas_call | solution.py:193
  22.1 4.3 %inner_0.1 = (f32[12,80,512]{2,1,0:T(8,128)S(1)}, s32[4]{0:T(128)S(1)}) custom-call(s32[4]{0:T(128)S(1)} %get-tuple-element.81.info, bf16[8,2,128,512]{3,2,1,0:T(8,128)(2,1)S(1)} %copy-done.1, bf16[8,2,128,512]{3,2,1,0:T(8,128)(2,1)S(1)} %collective-permute-done.sib, f32[1,512]{1,0:T(1,128)S(1)} %bitcast.11, ...), custom_call_target="tpu_custom_call" | custom-call | tf_op jit(solution)/shard_map/inner_0/pallas_call | solution.py:235
  27.9 3.2 %halo_0.1 = (bf16[12,80,512]{2,1,0:T(8,128)(2,1)S(1)}, bf16[12,80,512]{2,1,0:T(8,128)(2,1)S(1)}, s32[4]{0:T(128)S(1)}) custom-call(s32[4]{0:T(128)S(1)} %get-tuple-element.82.info, f32[12,80,512]{2,1,0:T(8,128)S(1)} %get-tuple-element.83.partial, bf16[6,88,512]{2,1,0:T(8,128)(2,1)S(1)} %collective-permute-done.3.refs_0_, ...), custom_call_target="tpu_custom_call" | custom-call | tf_op jit(solution)/shard_map/halo_0/pallas_call | solution.py:297
  31.1 2.1 %collective-permute-done.5.before = bf16[2,128,512]{2,1,0:T(8,128)(2,1)S(1)} collective-permute-done((bf16[2,128,512]{2,1,0:T(8,128)(2,1)S(1)}, bf16[2,128,512]{2,1,0:T(8,128)(2,1)S(1)}, u32[]{:S(2)}, u32[]{:S(2)}) %collective-permute-start.5) | collective-permute-done | bytes 262176 | tf_op jit(solution)/shard_map/ppermute | solution.py:36
  33.2 3.4 %temporal_0.1 = (bf16[16,80,512]{2,1,0:T(8,128)(2,1)S(1)}, bf16[1,80,512]{2,1,0:T(8,128)(2,1)S(1)}, bf16[15,80,512]{2,1,0:T(8,128)(2,1)S(1)}, s32[4]{0:T(128)S(1)}) custom-call(s32[4]{0:T(128)S(1)} %get-tuple-element.86.info, bf16[12,80,512]{2,1,0:T(8,128)(2,1)S(1)} %get-tuple-element.87.gated, bf16[4,128,512]{2,1,0:T(8,128)(2,1)S(1)} %get-tuple-element.88.edge_gated, ...), custom_call_target="tpu_custom_call" | custom-call | tf_op jit(solution)/shard_map/temporal_0/pallas_call | solution.py:348
  36.6 2.8 %collective-permute-start.6 = (bf16[6,40,512]{2,1,0:T(8,128)(2,1)S(1)}, bf16[6,40,512]{2,1,0:T(8,128)(2,1)S(1)}, u32[]{:S(2)}, u32[]{:S(2)}) collective-permute-start(bf16[6,40,512]{2,1,0:T(8,128)(2,1)S(1)} %get-tuple-element.94), channel_id=1, source_target_pairs={{0,1},{1,2},{2,3},{3,0},{4,7},{5,4},{6,5},{7,6},{8,9},{9,10},{10,1... | collective-permute-start | bytes 737288 | tf_op jit(solution)/shard_map/ppermute | solution.py:36
  39.6 2.8 %inner_1.1 = (f32[12,48,512]{2,1,0:T(8,128)S(1)}, s32[4]{0:T(128)S(1)}) custom-call(s32[4]{0:T(128)S(1)} %get-tuple-element.91.info, bf16[8,2,128,512]{3,2,1,0:T(8,128)(2,1)S(1)} %copy-done.1, bf16[8,2,128,512]{3,2,1,0:T(8,128)(2,1)S(1)} %collective-permute-done.sib, f32[1,512]{1,0:T(1,128)S(1)} %bitcast.13, ...), custom_call_target="tpu_custom_call" | custom-call | tf_op jit(solution)/shard_map/inner_1/pallas_call | solution.py:235
  42.4 2.2 %collective-permute-done.6.refs_1_ = bf16[6,40,512]{2,1,0:T(8,128)(2,1)S(1)} collective-permute-done((bf16[6,40,512]{2,1,0:T(8,128)(2,1)S(1)}, bf16[6,40,512]{2,1,0:T(8,128)(2,1)S(1)}, u32[]{:S(2)}, u32[]{:S(2)}) %collective-permute-start.6) | collective-permute-done | bytes 245792 | tf_op jit(solution)/shard_map/ppermute | solution.py:36
  45.4 2.5 %halo_1.1 = (bf16[12,48,512]{2,1,0:T(8,128)(2,1)S(1)}, bf16[12,48,512]{2,1,0:T(8,128)(2,1)S(1)}, s32[4]{0:T(128)S(1)}) custom-call(s32[4]{0:T(128)S(1)} %get-tuple-element.92.info, f32[12,48,512]{2,1,0:T(8,128)S(1)} %get-tuple-element.93.partial, bf16[6,88,512]{2,1,0:T(8,128)(2,1)S(1)} %collective-permute-done.3.refs_0_, ...), custom_call_target="tpu_custom_call" | custom-call | tf_op jit(solution)/shard_map/halo_1/pallas_call | solution.py:297
  47.9 2.6 %temporal_1.1 = (bf16[16,48,512]{2,1,0:T(8,128)(2,1)S(1)}, bf16[1,48,512]{2,1,0:T(8,128)(2,1)S(1)}, bf16[15,48,512]{2,1,0:T(8,128)(2,1)S(1)}, s32[4]{0:T(128)S(1)}) custom-call(s32[4]{0:T(128)S(1)} %get-tuple-element.96.info, bf16[12,48,512]{2,1,0:T(8,128)(2,1)S(1)} %get-tuple-element.97.gated, bf16[4,128,512]{2,1,0:T(8,128)(2,1)S(1)} %get-tuple-element.88.edge_gated, ...), custom_call_target="tpu_custom_call" | custom-call | tf_op jit(solution)/shard_map/temporal_1/pallas_call | solution.py:348
  52.0 3.1 %project_0.1 = (bf16[10,128,512]{2,1,0:T(8,128)(2,1)S(1)}, bf16[10,128,512]{2,1,0:T(8,128)(2,1)S(1)}, bf16[10,128,512]{2,1,0:T(8,128)(2,1)S(1)}, s32[4]{0:T(128)S(1)}) custom-call(s32[4]{0:T(128)S(1)} %get-tuple-element.99.info, bf16[1,80,512]{2,1,0:T(8,128)(2,1)S(1)} %get-tuple-element.100.n_first, bf16[15,80,512]{2,1,0:T(8,128)(2,1)S(1)} %get-tuple-element.101.n_rest, ...), custom_call_target="tpu_custom_call" | custom-call | tf_op jit(solution)/shard_map/project_0/pallas_call | solution.py:390
  55.1 2.1 %project_1.1 = (bf16[6,128,512]{2,1,0:T(8,128)(2,1)S(1)}, bf16[6,128,512]{2,1,0:T(8,128)(2,1)S(1)}, bf16[6,128,512]{2,1,0:T(8,128)(2,1)S(1)}, s32[4]{0:T(128)S(1)}) custom-call(s32[4]{0:T(128)S(1)} %get-tuple-element.102.info, bf16[1,48,512]{2,1,0:T(8,128)(2,1)S(1)} %get-tuple-element.103.n_first, bf16[15,48,512]{2,1,0:T(8,128)(2,1)S(1)} %get-tuple-element.104.n_rest, ...), custom_call_target="tpu_custom_call" | custom-call | tf_op jit(solution)/shard_map/project_1/pallas_call | solution.py:390
  57.3 9.3 %collective-permute-done.8.ctx = bf16[15,80,512]{2,1,0:T(8,128)(2,1)S(1)} collective-permute-done((bf16[15,80,512]{2,1,0:T(8,128)(2,1)S(1)}, bf16[15,80,512]{2,1,0:T(8,128)(2,1)S(1)}, u32[]{:S(2)}, u32[]{:S(2)}) %collective-permute-start.8) | collective-permute-done | bytes 1228832 | tf_op jit(solution)/shard_map/ppermute | solution.py:36
  66.6 6.5 %attend_0.1 = (bf16[2,2,80,512]{3,2,1,0:T(8,128)(2,1)S(1)}, bf16[2,2,80,512]{3,2,1,0:T(8,128)(2,1)S(1)}, bf16[2,2,80,512]{3,2,1,0:T(8,128)(2,1)S(1)}, bf16[2,2,80,512]{3,2,1,0:T(8,128)(2,1)S(1)}, s32[4]{0:T(128)S(1)}) custom-call(s32[4]{0:T(128)S(1)} %get-tuple-element.105.info, bf16[15,80,512]{2,1,0:T(8,128)(2,1)S(1)} %collective-permute-done.8.ctx, ...), custom_call_target="tpu_custom_call" | custom-call | tf_op jit(solution)/shard_map/attend_0/pallas_call | solution.py:464
  73.3 6.2 %collective-permute-start.11 = (bf16[2,2,80,512]{3,2,1,0:T(8,128)(2,1)S(1)}, bf16[2,2,80,512]{3,2,1,0:T(8,128)(2,1)S(1)}, u32[]{:S(2)}, u32[]{:S(2)}) collective-permute-start(bf16[2,2,80,512]{3,2,1,0:T(8,128)(2,1)S(1)} %get-tuple-element.118), channel_id=1, source_target_pairs={{0,2},{1,3},{2,0},{3,1},{4,6},{5,7},{6,4},{7,5},{8,10},{9,11},{10,... | collective-permute-start | bytes 983048 | tf_op jit(solution)/shard_map/ppermute | solution.py:36
  79.6 2.8 %collective-permute-done.9.ctx = bf16[15,48,512]{2,1,0:T(8,128)(2,1)S(1)} collective-permute-done((bf16[15,48,512]{2,1,0:T(8,128)(2,1)S(1)}, bf16[15,48,512]{2,1,0:T(8,128)(2,1)S(1)}, u32[]{:S(2)}, u32[]{:S(2)}) %collective-permute-start.9) | collective-permute-done | bytes 737312 | tf_op jit(solution)/shard_map/ppermute | solution.py:36
  82.4 5.0 %attend_1.1 = (bf16[2,2,48,512]{3,2,1,0:T(8,128)(2,1)S(1)}, bf16[2,2,48,512]{3,2,1,0:T(8,128)(2,1)S(1)}, bf16[2,2,48,512]{3,2,1,0:T(8,128)(2,1)S(1)}, bf16[2,2,48,512]{3,2,1,0:T(8,128)(2,1)S(1)}, s32[4]{0:T(128)S(1)}) custom-call(s32[4]{0:T(128)S(1)} %get-tuple-element.110.info, bf16[15,48,512]{2,1,0:T(8,128)(2,1)S(1)} %collective-permute-done.9.ctx, ...), custom_call_target="tpu_custom_call" | custom-call | tf_op jit(solution)/shard_map/attend_1/pallas_call | solution.py:464
  87.6 6.2 %collective-permute-start.14 = (bf16[2,2,48,512]{3,2,1,0:T(8,128)(2,1)S(1)}, bf16[2,2,48,512]{3,2,1,0:T(8,128)(2,1)S(1)}, u32[]{:S(2)}, u32[]{:S(2)}) collective-permute-start(bf16[2,2,48,512]{3,2,1,0:T(8,128)(2,1)S(1)} %get-tuple-element.124), channel_id=1, source_target_pairs={{0,2},{1,3},{2,0},{3,1},{4,6},{5,7},{6,4},{7,5},{8,10},{9,11},{10,... | collective-permute-start | bytes 589832 | tf_op jit(solution)/shard_map/ppermute | solution.py:36
  95.2 4.4 %collective-permute-done.13.refs_1_ = bf16[2,2,48,512]{3,2,1,0:T(8,128)(2,1)S(1)} collective-permute-done((bf16[2,2,48,512]{3,2,1,0:T(8,128)(2,1)S(1)}, bf16[2,2,48,512]{3,2,1,0:T(8,128)(2,1)S(1)}, u32[]{:S(2)}, u32[]{:S(2)}) %collective-permute-start.13) | collective-permute-done | bytes 196640 | tf_op jit(solution)/shard_map/ppermute | solution.py:36
  99.6 3.0 %collective-permute-done.14.refs_2_ = bf16[2,2,48,512]{3,2,1,0:T(8,128)(2,1)S(1)} collective-permute-done((bf16[2,2,48,512]{3,2,1,0:T(8,128)(2,1)S(1)}, bf16[2,2,48,512]{3,2,1,0:T(8,128)(2,1)S(1)}, u32[]{:S(2)}, u32[]{:S(2)}) %collective-permute-start.14) | collective-permute-done | bytes 196640 | tf_op jit(solution)/shard_map/ppermute | solution.py:36
  105.5 2.3 %place_0.1 = (bf16[2,8,128,512]{3,2,1,0:T(8,128)(2,1)}, s32[4]{0:T(128)S(1)}) custom-call(s32[4]{0:T(128)S(1)} %get-tuple-element.129.info, bf16[2,2,80,512]{3,2,1,0:T(8,128)(2,1)S(1)} %get-tuple-element.116.refs_0_, bf16[2,2,80,512]{3,2,1,0:T(8,128)(2,1)S(1)} %collective-permute-done.10.refs_1_, ...), custom_call_target="tpu_custom_call" | custom-call | tf_op jit(solution)/shard_map/place_0/pallas_call | solution.py:521
  (53 shorter events, 20.3 us)
Async XLA Ops:
  0.0 16.4 %collective-permute-start = (bf16[8,2,128,512]{3,2,1,0:T(8,128)(2,1)}, bf16[8,2,128,512]{3,2,1,0:T(8,128)(2,1)S(1)}, u32[]{:S(2)}, u32[]{:S(2)}) collective-permute-start(bf16[8,2,128,512]{3,2,1,0:T(8,128)(2,1)} %own.5), channel_id=1, source_target_pairs={{0,4},{1,5},{2,6},{3,7},{4,0},{5,1},{6,2},{7,3},{8,12},{9,13},{10,... | collective-permute-start | bytes 6291464 | tf_op jit(solution)/shard_map/ppermute | solution.py:36
  4.2 8.0 %collective-permute-start.1 = (bf16[2,128,512]{2,1,0:T(8,128)(2,1)S(1)}, bf16[2,128,512]{2,1,0:T(8,128)(2,1)S(1)}, u32[]{:S(2)}, u32[]{:S(2)}) collective-permute-start(bf16[2,128,512]{2,1,0:T(8,128)(2,1)S(1)} %get-tuple-element.76), channel_id=1, source_target_pairs={{0,1},{1,2},{2,3},{3,0},{4,7},{5,4},{6,5},{7,6},{8,9},{9,10},{10,1... | collective-permute-start | bytes 786440 | tf_op jit(solution)/shard_map/ppermute | solution.py:36
  7.1 6.1 %collective-permute-start.2 = (bf16[2,128,512]{2,1,0:T(8,128)(2,1)S(1)}, bf16[2,128,512]{2,1,0:T(8,128)(2,1)S(1)}, u32[]{:S(2)}, u32[]{:S(2)}) collective-permute-start(bf16[2,128,512]{2,1,0:T(8,128)(2,1)S(1)} %get-tuple-element.77), channel_id=1, source_target_pairs={{0,7},{1,4},{2,5},{3,6},{4,1},{5,2},{6,3},{7,0},{8,15},{9,12},{10,... | collective-permute-start | bytes 786440 | tf_op jit(solution)/shard_map/ppermute | solution.py:36
  9.5 6.9 %copy-start.8 = (f32[512]{0:T(512)S(1)}, f32[512]{0:T(512)}, u32[]{:S(2)}) copy-start(f32[512]{0:T(512)} %param.11) | copy-start | bytes 6148
  9.5 6.9 %copy-start.9 = (f32[512]{0:T(512)S(1)}, f32[512]{0:T(512)}, u32[]{:S(2)}) copy-start(f32[512]{0:T(512)} %param.13) | copy-start | bytes 6148
  13.2 14.7 %collective-permute-start.3 = (bf16[6,88,512]{2,1,0:T(8,128)(2,1)S(1)}, bf16[6,88,512]{2,1,0:T(8,128)(2,1)S(1)}, u32[]{:S(2)}, u32[]{:S(2)}) collective-permute-start(bf16[6,88,512]{2,1,0:T(8,128)(2,1)S(1)} %get-tuple-element.84), channel_id=1, source_target_pairs={{0,1},{1,2},{2,3},{3,0},{4,7},{5,4},{6,5},{7,6},{8,9},{9,10},{10,1... | collective-permute-start | bytes 1622024 | tf_op jit(solution)/shard_map/ppermute | solution.py:36
  16.4 11.5 %collective-permute-start.4 = (bf16[6,88,512]{2,1,0:T(8,128)(2,1)S(1)}, bf16[6,88,512]{2,1,0:T(8,128)(2,1)S(1)}, u32[]{:S(2)}, u32[]{:S(2)}) collective-permute-start(bf16[6,88,512]{2,1,0:T(8,128)(2,1)S(1)} %get-tuple-element.85), channel_id=1, source_target_pairs={{0,7},{1,4},{2,5},{3,6},{4,1},{5,2},{6,3},{7,0},{8,15},{9,12},{10,... | collective-permute-start | bytes 1622024 | tf_op jit(solution)/shard_map/ppermute | solution.py:36
  20.7 12.5 %collective-permute-start.5 = (bf16[2,128,512]{2,1,0:T(8,128)(2,1)S(1)}, bf16[2,128,512]{2,1,0:T(8,128)(2,1)S(1)}, u32[]{:S(2)}, u32[]{:S(2)}) collective-permute-start(bf16[2,128,512]{2,1,0:T(8,128)(2,1)S(1)} %slice.3), channel_id=1, source_target_pairs={{0,8},{1,9},{2,10},{3,11},{4,12},{5,13},{6,14},{7,15},{8,16},{9,17... | collective-permute-start | bytes 786440 | tf_op jit(solution)/shard_map/ppermute | solution.py:36
  27.9 5.3 %copy-start.4 = (bf16[3,512,512]{2,1,0:T(8,128)(2,1)S(1)}, bf16[3,512,512]{2,1,0:T(8,128)(2,1)}, u32[]{:S(2)}) copy-start(bf16[3,512,512]{2,1,0:T(8,128)(2,1)} %w.3) | copy-start | bytes 4718596
  27.9 5.3 %copy-start.10 = (f32[512]{0:T(512)S(1)}, f32[512]{0:T(512)}, u32[]{:S(2)}) copy-start(f32[512]{0:T(512)} %param.15) | copy-start | bytes 6148
  36.6 30.0 %collective-permute-start.8 = (bf16[15,80,512]{2,1,0:T(8,128)(2,1)S(1)}, bf16[15,80,512]{2,1,0:T(8,128)(2,1)S(1)}, u32[]{:S(2)}, u32[]{:S(2)}) collective-permute-start(bf16[15,80,512]{2,1,0:T(8,128)(2,1)S(1)} %get-tuple-element.101.n_rest), channel_id=1, source_target_pairs={{0,8},{1,9},{2,10},{3,11},{4,12},{5,13},{6,14},{7,15},{8,16},{9,17... | collective-permute-start | bytes 3686408 | tf_op jit(solution)/shard_map/ppermute | solution.py:36
  36.6 8.0 %collective-permute-start.6 = (bf16[6,40,512]{2,1,0:T(8,128)(2,1)S(1)}, bf16[6,40,512]{2,1,0:T(8,128)(2,1)S(1)}, u32[]{:S(2)}, u32[]{:S(2)}) collective-permute-start(bf16[6,40,512]{2,1,0:T(8,128)(2,1)S(1)} %get-tuple-element.94), channel_id=1, source_target_pairs={{0,1},{1,2},{2,3},{3,0},{4,7},{5,4},{6,5},{7,6},{8,9},{9,10},{10,1... | collective-permute-start | bytes 737288 | tf_op jit(solution)/shard_map/ppermute | solution.py:36
  39.4 5.9 %collective-permute-start.7 = (bf16[6,40,512]{2,1,0:T(8,128)(2,1)S(1)}, bf16[6,40,512]{2,1,0:T(8,128)(2,1)S(1)}, u32[]{:S(2)}, u32[]{:S(2)}) collective-permute-start(bf16[6,40,512]{2,1,0:T(8,128)(2,1)S(1)} %get-tuple-element.95), channel_id=1, source_target_pairs={{0,7},{1,4},{2,5},{3,6},{4,1},{5,2},{6,3},{7,0},{8,15},{9,12},{10,... | collective-permute-start | bytes 737288 | tf_op jit(solution)/shard_map/ppermute | solution.py:36
  47.8 4.2 %copy-start.2 = (bf16[512,512]{1,0:T(8,128)(2,1)S(1)}, bf16[512,512]{1,0:T(8,128)(2,1)}, u32[]{:S(2)}) copy-start(bf16[512,512]{1,0:T(8,128)(2,1)} %wk.7) | copy-start | bytes 1572868
  50.5 31.9 %collective-permute-start.9 = (bf16[15,48,512]{2,1,0:T(8,128)(2,1)S(1)}, bf16[15,48,512]{2,1,0:T(8,128)(2,1)S(1)}, u32[]{:S(2)}, u32[]{:S(2)}) collective-permute-start(bf16[15,48,512]{2,1,0:T(8,128)(2,1)S(1)} %get-tuple-element.104.n_rest), channel_id=1, source_target_pairs={{0,8},{1,9},{2,10},{3,11},{4,12},{5,13},{6,14},{7,15},{8,16},{9,17... | collective-permute-start | bytes 2211848 | tf_op jit(solution)/shard_map/ppermute | solution.py:36
  55.1 11.5 %copy-start.7 = (bf16[512,512]{1,0:T(8,128)(2,1)S(1)}, bf16[512,512]{1,0:T(8,128)(2,1)}, u32[]{:S(2)}) copy-start(bf16[512,512]{1,0:T(8,128)(2,1)} %wo.3) | copy-start | bytes 1572868
  73.1 20.6 %collective-permute-start.10 = (bf16[2,2,80,512]{3,2,1,0:T(8,128)(2,1)S(1)}, bf16[2,2,80,512]{3,2,1,0:T(8,128)(2,1)S(1)}, u32[]{:S(2)}, u32[]{:S(2)}) collective-permute-start(bf16[2,2,80,512]{3,2,1,0:T(8,128)(2,1)S(1)} %get-tuple-element.117), channel_id=1, source_target_pairs={{0,1},{1,2},{2,3},{3,0},{4,5},{5,6},{6,7},{7,4},{8,9},{9,10},{10,1... | collective-permute-start | bytes 983048 | tf_op jit(solution)/shard_map/ppermute | solution.py:36
  73.3 20.7 %collective-permute-start.11 = (bf16[2,2,80,512]{3,2,1,0:T(8,128)(2,1)S(1)}, bf16[2,2,80,512]{3,2,1,0:T(8,128)(2,1)S(1)}, u32[]{:S(2)}, u32[]{:S(2)}) collective-permute-start(bf16[2,2,80,512]{3,2,1,0:T(8,128)(2,1)S(1)} %get-tuple-element.118), channel_id=1, source_target_pairs={{0,2},{1,3},{2,0},{3,1},{4,6},{5,7},{6,4},{7,5},{8,10},{9,11},{10,... | collective-permute-start | bytes 983048 | tf_op jit(solution)/shard_map/ppermute | solution.py:36
  79.6 14.5 %collective-permute-start.12 = (bf16[2,2,80,512]{3,2,1,0:T(8,128)(2,1)S(1)}, bf16[2,2,80,512]{3,2,1,0:T(8,128)(2,1)S(1)}, u32[]{:S(2)}, u32[]{:S(2)}) collective-permute-start(bf16[2,2,80,512]{3,2,1,0:T(8,128)(2,1)S(1)} %get-tuple-element.119), channel_id=1, source_target_pairs={{0,3},{1,0},{2,1},{3,2},{4,7},{5,4},{6,5},{7,6},{8,11},{9,8},{10,9... | collective-permute-start | bytes 983048 | tf_op jit(solution)/shard_map/ppermute | solution.py:36
  87.4 12.2 %collective-permute-start.13 = (bf16[2,2,48,512]{3,2,1,0:T(8,128)(2,1)S(1)}, bf16[2,2,48,512]{3,2,1,0:T(8,128)(2,1)S(1)}, u32[]{:S(2)}, u32[]{:S(2)}) collective-permute-start(bf16[2,2,48,512]{3,2,1,0:T(8,128)(2,1)S(1)} %get-tuple-element.123), channel_id=1, source_target_pairs={{0,1},{1,2},{2,3},{3,0},{4,5},{5,6},{6,7},{7,4},{8,9},{9,10},{10,1... | collective-permute-start | bytes 589832 | tf_op jit(solution)/shard_map/ppermute | solution.py:36
  87.6 15.0 %collective-permute-start.14 = (bf16[2,2,48,512]{3,2,1,0:T(8,128)(2,1)S(1)}, bf16[2,2,48,512]{3,2,1,0:T(8,128)(2,1)S(1)}, u32[]{:S(2)}, u32[]{:S(2)}) collective-permute-start(bf16[2,2,48,512]{3,2,1,0:T(8,128)(2,1)S(1)} %get-tuple-element.124), channel_id=1, source_target_pairs={{0,2},{1,3},{2,0},{3,1},{4,6},{5,7},{6,4},{7,5},{8,10},{9,11},{10,... | collective-permute-start | bytes 589832 | tf_op jit(solution)/shard_map/ppermute | solution.py:36
  93.7 8.8 %collective-permute-start.15 = (bf16[2,2,48,512]{3,2,1,0:T(8,128)(2,1)S(1)}, bf16[2,2,48,512]{3,2,1,0:T(8,128)(2,1)S(1)}, u32[]{:S(2)}, u32[]{:S(2)}) collective-permute-start(bf16[2,2,48,512]{3,2,1,0:T(8,128)(2,1)S(1)} %get-tuple-element.125), channel_id=1, source_target_pairs={{0,3},{1,0},{2,1},{3,2},{4,7},{5,4},{6,5},{7,6},{8,11},{9,8},{10,9... | collective-permute-start | bytes 589832 | tf_op jit(solution)/shard_map/ppermute | solution.py:36
  102.6 3.0 %collective-permute-start.16 = (bf16[4,2,80,512]{3,2,1,0:T(8,128)(2,1)S(1)}, bf16[4,2,80,512]{3,2,1,0:T(8,128)(2,1)S(1)}, u32[]{:S(2)}, u32[]{:S(2)}) collective-permute-start(bf16[4,2,80,512]{3,2,1,0:T(8,128)(2,1)S(1)} %get-tuple-element.130), channel_id=1, source_target_pairs={{0,4},{1,5},{2,6},{3,7},{4,0},{5,1},{6,2},{7,3},{8,12},{9,13},{10,... | collective-permute-start | bytes 1966088 | tf_op jit(solution)/shard_map/ppermute | solution.py:36
  104.9 2.8 %collective-permute-start.17 = (bf16[4,2,48,512]{3,2,1,0:T(8,128)(2,1)S(1)}, bf16[4,2,48,512]{3,2,1,0:T(8,128)(2,1)S(1)}, u32[]{:S(2)}, u32[]{:S(2)}) collective-permute-start(bf16[4,2,48,512]{3,2,1,0:T(8,128)(2,1)S(1)} %get-tuple-element.132), channel_id=1, source_target_pairs={{0,4},{1,5},{2,6},{3,7},{4,0},{5,1},{6,2},{7,3},{8,12},{9,13},{10,... | collective-permute-start | bytes 1179656 | tf_op jit(solution)/shard_map/ppermute | solution.py:36
  (5 other events, 16.4 us)

commit v2 on v1

--- a/solution.py
+++ b/solution.py
@@ -15,7 +15,8 @@
 RIM = 8
 EDGE = 2
 MAIN = 8 - EDGE
-CUTS = (0, 80, 128)
+CUTS = (0, 64, 128)
+RING = 16
 ORDER = ("e0", "i0", "s0", "t0", "i1", "s1", "t1", "p0", "p1", "a0", "a1", "d0", "d1", "w0", "w1")
 AXES = ("frames", "rows")
 F32 = jnp.float32
@@ -58,6 +59,16 @@
 
 
 INFO = jax.ShapeDtypeStruct((4,), jnp.int32)
+
+
+def to_chip_before(f, r):
+    core, x = f % 2, f // 2 % 4
+    return f // 8 * 8 + (x - 1) % 4 * 2 + core, r
+
+
+def to_chip_before_last(f, r):
+    to_f, _ = to_chip_before(f, r)
+    return (to_f + 8 if f // 2 % 4 == 1 else to_f), r
 
 
 def rms(v, gain):
@@ -104,9 +115,9 @@
 
 def gate_into(mixed, gated, at, total, gain):
     one = total.astype(BF16)
-    normed = rms(one.astype(F32), gain)
+    half = rms(one.astype(F32), gain * 0.5)
     mixed[at] = one
-    gated[at] = (normed / (1.0 + jnp.exp(-normed))).astype(BF16)
+    gated[at] = (half + half * jnp.tanh(half)).astype(BF16)
 
 
 def first_rows_kernel(info, latents, outer, inner, info_out):
@@ -209,7 +220,7 @@
     wc = c1 - c0
     k = info[0]
     gain = g1[...]
-    step = frames_per_step(MAIN, wc, 300)
+    step = frames_per_step(MAIN, wc, 500)
 
     def prepare(index, role):
         for i in range(step):
@@ -237,7 +248,7 @@
         out_shape=(jax.ShapeDtypeStruct((2 * MAIN, wc, C), F32), INFO),
         in_specs=[SMEM, VMEM, VMEM, VMEM, VMEM],
         out_specs=(VMEM, SMEM),
-        scratch_shapes=[pltpu.VMEM((2, 2, frames_per_step(MAIN, wc, 300) * wc, 3 * C), BF16)],
+        scratch_shapes=[pltpu.VMEM((2, 2, frames_per_step(MAIN, wc, 500) * wc, 3 * C), BF16)],
         compiler_params=pltpu.CompilerParams(vmem_limit_bytes=20 * 2**20),
         cost_estimate=LIGHT,
         name=f"inner_{j}",
@@ -256,7 +267,7 @@
     first = j + 1 - n_pieces
     gain_one = g1[...] * info[2].astype(F32)
     gain_two = g2[...]
-    step = frames_per_step(MAIN, wc, 300)
+    step = frames_per_step(MAIN, wc, 500)
 
     def prepare(index):
         for i in range(step):
@@ -299,11 +310,25 @@
         out_shape=(shape, shape, INFO),
         in_specs=[SMEM] + [VMEM] * (2 * n + 4),
         out_specs=(VMEM, VMEM, SMEM),
-        scratch_shapes=[pltpu.VMEM((2, frames_per_step(MAIN, wc, 300) * wc, 3 * C), BF16)],
+        scratch_shapes=[pltpu.VMEM((2, frames_per_step(MAIN, wc, 500) * wc, 3 * C), BF16)],
         compiler_params=pltpu.CompilerParams(vmem_limit_bytes=18 * 2**20),
         cost_estimate=LIGHT,
         name=f"halo_{j}",
     )(info, partial, *same, *cross, g1, g2, wv)
+
+
+def split_columns(j):
+    wc = CUTS[j + 1] - CUTS[j]
+    ring = RING if j == len(CUTS) - 2 else 0
+    return (wc - ring, ring) if ring else (wc,)
+
+
+def frames_into(x, wc, arrays):
+    for f in range(NF - 1):
+        at = (f + 1) * wc
+        for array in arrays:
+            x[at : at + array.shape[1]] = array[f]
+            at += array.shape[1]
 
 
 def place_of(f):
@@ -312,7 +337,7 @@
 
 
 def temporal_kernel(j, info, gated, edge_gated, before, mixed, edge_mixed, w, g3, *refs):
-    mixed_two, n_first, n_rest, info_out, x = refs
+    mixed_two, n_first, *n_rest, info_out, x = refs
     pass_on(info, info_out)
     c0, c1 = CUTS[j], CUTS[j + 1]
     wc = c1 - c0
@@ -340,7 +365,10 @@
             if f == 0:
                 n_first[0] = normed
             else:
-                n_rest[f - 1] = normed
+                at = 0
+                for part in n_rest:
+                    part[f - 1] = normed[at : at + part.shape[1]]
+                    at += part.shape[1]
 
 
 def temporal_stage(j, info, gated, edge_gated, before, mixed, edge_mixed, w, g3):
@@ -350,11 +378,11 @@
         out_shape=(
             jax.ShapeDtypeStruct((NF, wc, C), BF16),
             jax.ShapeDtypeStruct((1, wc, C), BF16),
-            jax.ShapeDtypeStruct((NF - 1, wc, C), BF16),
+            *(jax.ShapeDtypeStruct((NF - 1, n, C), BF16) for n in split_columns(j)),
             INFO,
         ),
         in_specs=[SMEM] + [VMEM] * 7,
-        out_specs=(VMEM, VMEM, VMEM, SMEM),
+        out_specs=(VMEM,) * (2 + len(split_columns(j))) + (SMEM,),
         scratch_shapes=[pltpu.VMEM(((NF + 2) * wc, C), BF16)],
         compiler_params=pltpu.CompilerParams(vmem_limit_bytes=16 * 2**20),
         cost_estimate=LIGHT,
@@ -370,10 +398,11 @@
         dst[g, frame * 8 : frame * 8 + 16, :] = pair.astype(BF16)
 
 
-def qkv_kernel(wc, info, n_first, n_rest, wq, wk, wv, q, k, v, info_out, x):
+def qkv_kernel(wc, count, info, n_first, *refs):
+    n_rest, (wq, wk, wv, q, k, v, info_out, x) = refs[:count], refs[count:]
     pass_on(info, info_out)
     x[0:wc] = n_first[0]
-    x[wc:] = n_rest[...].reshape((NF - 1) * wc, C)
+    frames_into(x, wc, n_rest)
     for f0 in range(0, NF, 4):
         rows = x[f0 * wc : (f0 + 4) * wc, :]
         for w, dst, scale in ((wq, q, 0.125), (wk, k, None), (wv, v, None)):
@@ -388,24 +417,25 @@
     wc = CUTS[j + 1] - CUTS[j]
     shape = jax.ShapeDtypeStruct((wc // 8, NF * 8, C), BF16)
     return pl.pallas_call(
-        functools.partial(qkv_kernel, wc),
+        functools.partial(qkv_kernel, wc, len(n_rest)),
         out_shape=(shape, shape, shape, INFO),
-        in_specs=[SMEM] + [VMEM] * 5,
+        in_specs=[SMEM] + [VMEM] * (4 + len(n_rest)),
         out_specs=(VMEM, VMEM, VMEM, SMEM),
         scratch_shapes=[pltpu.VMEM((NF * wc, C), BF16)],
         compiler_params=pltpu.CompilerParams(vmem_limit_bytes=20 * 2**20),
         cost_estimate=LIGHT,
         name=f"project_{j}",
-    )(info, n_first, n_rest, wq, wk, wv)
-
-
-def attend_kernel(wc, info, ctx, wk, wv, wo, q, k, v, mixed_two, *refs):
-    blocks, (info_out, x, kc, vc, att, out) = refs[:4], refs[4:]
+    )(info, n_first, *n_rest, wq, wk, wv)
+
+
+def attend_kernel(wc, count, info, *refs):
+    ctx, refs = refs[:count], refs[count:]
+    wk, wv, wo, q, k, v, mixed_two, *blocks, info_out, x, kc, vc, att, out = refs
     pass_on(info, info_out)
     groups = wc // 8
     rows = NF * 8
     x[0:wc] = jnp.zeros((wc, C), BF16)
-    x[wc:] = ctx[...].reshape((NF - 1) * wc, C)
+    frames_into(x, wc, ctx)
     for f0 in range(0, NF, 4):
         part = x[f0 * wc : (f0 + 4) * wc, :]
         for w, dst in ((wk, kc), (wv, vc)):
@@ -462,9 +492,9 @@
     wc = CUTS[j + 1] - CUTS[j]
     groups = wc // 8
     return pl.pallas_call(
-        functools.partial(attend_kernel, wc),
+        functools.partial(attend_kernel, wc, len(ctx)),
         out_shape=(jax.ShapeDtypeStruct((2, 2, wc, C), BF16),) * 4 + (INFO,),
-        in_specs=[SMEM] + [VMEM] * 8,
+        in_specs=[SMEM] + [VMEM] * (7 + len(ctx)),
         out_specs=(VMEM,) * 4 + (SMEM,),
         scratch_shapes=[
             pltpu.VMEM((NF * wc, C), BF16),
@@ -476,7 +506,7 @@
         compiler_params=pltpu.CompilerParams(vmem_limit_bytes=20 * 2**20),
         cost_estimate=LIGHT,
         name=f"attend_{j}",
-    )(info, ctx, wk, wv, wo, q, k, v, mixed_two)
+    )(info, *ctx, wk, wv, wo, q, k, v, mixed_two)
 
 
 def deal_kernel(info, *refs):
@@ -584,7 +614,7 @@
 
     def temporal(j, info):
         s = state[j]
-        s["mixed"], s["first"], s["rest"], info = temporal_stage(
+        s["mixed"], s["first"], *s["rest"], info = temporal_stage(
             j,
             info,
             s["gated"],
@@ -595,7 +625,9 @@
             temporal_weight,
             g3,
         )
-        s["ctx"] = routed(s["rest"], to_next_chip)
+        s["ctx"] = [routed(s["rest"][0], to_next_chip)]
+        if len(s["rest"]) > 1:
+            s["ctx"].append(routed(s["rest"][1], to_chip_before))
         return info
 
     def project(j, info):
@@ -603,6 +635,9 @@
         s["q"], s["k"], s["v"], info = qkv_stage(
             j, info, s["first"], s["rest"], query_weight, key_weight, value_weight
         )
+        if len(s["ctx"]) > 1:
+            hop, s["q"] = lax.optimization_barrier((s["ctx"][1], s["q"]))
+            s["ctx"][1] = routed(hop, to_chip_before)
         return info
 
     def attend(j, info):
@@ -619,6 +654,10 @@
             s["v"],
             s["mixed"],
         )
+        ring = state[-1]["ctx"]
+        if j + 2 == len(state) and len(ring) > 1:
+            hop, blocks[0] = lax.optimization_barrier((ring[1], blocks[0]))
+            ring[1] = routed(hop, to_chip_before_last)
         for n in (2, 1, 3):
             blocks[n] = routed(blocks[n], lambda f, r: (f, r + n))
         s["blocks"] = blocks

time: 110 us -> 109 us (level)
  waiting for transfers between devices: 29 us -> 24 us
  starting transfers between devices: 27.7 us -> 32.6 us
  Pallas kernels: 48.8 us -> 47.3 us
    ppermute x18 -> x21, waiting for transfers between devices: 29 us -> 24 us  [routed(): return lax.ppermute(x, AXES, pairs)]
    ppermute x18 -> x21, starting transfers between devices: 27.7 us -> 32.6 us  [routed(): return lax.ppermute(x, AXES, pairs)]
  transfers between devices with their start and end apart: 18 -> 21, of which waited for: 12 -> 9; matrix products, arithmetic and copies ran while one was open for 0% -> 0% of each run, Pallas kernels for 40% -> 39%
where the time goes in v2:
time: 109 us; the launch traced here: 108 us
  Pallas kernels  47.3 us (43%)
  starting transfers between devices  32.6 us (30%)
  waiting for transfers between devices  24 us (22%)
  local copies, waits for them, and re-layouts  3.99 us (4%)
    ppermute x21, starting transfers between devices, routed(): return lax.ppermute(x, AXES, pairs)  32.6 us
    ppermute x21, waiting for transfers between devices, routed(): return lax.ppermute(x, AXES, pairs)  24 us
    pallas_call x2, Pallas kernels, attend_stage(): pl.pallas_call(functools.partial(attend_kernel, wc, len(ctx)), out_shape=...  11.5 us
    pallas_call x2, Pallas kernels, inner_stage(): pl.pallas_call(functools.partial(inner_kernel, j), out_shape=(jax.ShapeDt...  6.53 us
    pallas_call x2, Pallas kernels, qkv_stage(): pl.pallas_call(functools.partial(qkv_kernel, wc, len(n_rest)), out_shape=...  5.62 us
    pallas_call x2, Pallas kernels, temporal_stage(): pl.pallas_call(functools.partial(temporal_kernel, j), out_shape=(jax.Shap...  5.48 us
    pallas_call x2, Pallas kernels, halo_stage(): pl.pallas_call(functools.partial(halo_kernel, j, n), out_shape=(shape, sh...  5.08 us
    pallas_call x2, Pallas kernels, place_stage(): pl.pallas_call(functools.partial(place_kernel, j), out_shape=(jax.ShapeDt...  4.26 us
  transfers between devices with their start and end apart: 21, of which 9 were waited for; matrix products, arithmetic and copies ran while one was open for 0% of the time, Pallas kernels for 39%

profile of v2, /device:TPU:1, one launch (start us, length us, event | category | flops | bytes accessed | tf_op | source)
XLA Modules:
  0.0 108.3 jit_solution(8220315583311437858)
XLA Ops:
  4.2 2.9 %collective-permute-start.1 = (bf16[2,128,512]{2,1,0:T(8,128)(2,1)S(1)}, bf16[2,128,512]{2,1,0:T(8,128)(2,1)S(1)}, u32[]{:S(2)}, u32[]{:S(2)}) collective-permute-start(bf16[2,128,512]{2,1,0:T(8,128)(2,1)S(1)} %get-tuple-element.81), channel_id=1, source_target_pairs={{0,1},{1,2},{2,3},{3,0},{4,7},{5,4},{6,5},{7,6},{8,9},{9,10},{10,1... | collective-permute-start | bytes 786440 | tf_op jit(solution)/shard_map/ppermute | solution.py:37
  7.2 2.3 %copy-done.5 = bf16[3,3,512,512]{3,2,1,0:T(8,128)(2,1)S(1)} copy-done((bf16[3,3,512,512]{3,2,1,0:T(8,128)(2,1)S(1)}, bf16[3,3,512,512]{3,2,1,0:T(8,128)(2,1)}, u32[]{:S(2)}) %copy-start.5) | copy-done | bytes 4718616
  13.2 3.1 %collective-permute-start.3 = (bf16[6,72,512]{2,1,0:T(8,128)(2,1)S(1)}, bf16[6,72,512]{2,1,0:T(8,128)(2,1)S(1)}, u32[]{:S(2)}, u32[]{:S(2)}) collective-permute-start(bf16[6,72,512]{2,1,0:T(8,128)(2,1)S(1)} %get-tuple-element.89), channel_id=1, source_target_pairs={{0,1},{1,2},{2,3},{3,0},{4,7},{5,4},{6,5},{7,6},{8,9},{9,10},{10,1... | collective-permute-start | bytes 1327112 | tf_op jit(solution)/shard_map/ppermute | solution.py:37
  16.4 3.8 %edge.1 = (bf16[4,128,512]{2,1,0:T(8,128)(2,1)S(1)}, bf16[4,128,512]{2,1,0:T(8,128)(2,1)S(1)}, s32[4]{0:T(128)S(1)}) custom-call(s32[4]{0:T(128)S(1)} %get-tuple-element.76.info, bf16[8,2,128,512]{3,2,1,0:T(8,128)(2,1)S(1)} %copy-done.1, bf16[8,2,128,512]{3,2,1,0:T(8,128)(2,1)S(1)} %collective-permute-done.sib, ...), custom_call_target="tpu_custom_call" | custom-call | tf_op jit(solution)/shard_map/edge/pallas_call | solution.py:204
  21.5 3.3 %inner_0.1 = (f32[12,64,512]{2,1,0:T(8,128)S(1)}, s32[4]{0:T(128)S(1)}) custom-call(s32[4]{0:T(128)S(1)} %get-tuple-element.86.info, bf16[8,2,128,512]{3,2,1,0:T(8,128)(2,1)S(1)} %copy-done.1, bf16[8,2,128,512]{3,2,1,0:T(8,128)(2,1)S(1)} %collective-permute-done.sib, f32[1,512]{1,0:T(1,128)S(1)} %bitcast.11, ...), custom_call_target="tpu_custom_call" | custom-call | tf_op jit(solution)/shard_map/inner_0/pallas_call | solution.py:246
  25.8 2.5 %halo_0.1 = (bf16[12,64,512]{2,1,0:T(8,128)(2,1)S(1)}, bf16[12,64,512]{2,1,0:T(8,128)(2,1)S(1)}, s32[4]{0:T(128)S(1)}) custom-call(s32[4]{0:T(128)S(1)} %get-tuple-element.87.info, f32[12,64,512]{2,1,0:T(8,128)S(1)} %get-tuple-element.88.partial, bf16[6,72,512]{2,1,0:T(8,128)(2,1)S(1)} %collective-permute-done.3.refs_0_, ...), custom_call_target="tpu_custom_call" | custom-call | tf_op jit(solution)/shard_map/halo_0/pallas_call | solution.py:308
  28.4 4.2 %collective-permute-done.5.before = bf16[2,128,512]{2,1,0:T(8,128)(2,1)S(1)} collective-permute-done((bf16[2,128,512]{2,1,0:T(8,128)(2,1)S(1)}, bf16[2,128,512]{2,1,0:T(8,128)(2,1)S(1)}, u32[]{:S(2)}, u32[]{:S(2)}) %collective-permute-start.5) | collective-permute-done | bytes 262176 | tf_op jit(solution)/shard_map/ppermute | solution.py:37
  32.6 3.0 %temporal_0.1 = (bf16[16,64,512]{2,1,0:T(8,128)(2,1)S(1)}, bf16[1,64,512]{2,1,0:T(8,128)(2,1)S(1)}, bf16[15,64,512]{2,1,0:T(8,128)(2,1)S(1)}, s32[4]{0:T(128)S(1)}) custom-call(s32[4]{0:T(128)S(1)} %get-tuple-element.91.info, bf16[12,64,512]{2,1,0:T(8,128)(2,1)S(1)} %get-tuple-element.92.gated, bf16[4,128,512]{2,1,0:T(8,128)(2,1)S(1)} %get-tuple-element.93.edge_gated, ...), custom_call_target="tpu_custom_call" | custom-call | tf_op jit(solution)/shard_map/temporal_0/pallas_call | solution.py:376
  37.4 3.3 %inner_1.1 = (f32[12,64,512]{2,1,0:T(8,128)S(1)}, s32[4]{0:T(128)S(1)}) custom-call(s32[4]{0:T(128)S(1)} %get-tuple-element.96.info, bf16[8,2,128,512]{3,2,1,0:T(8,128)(2,1)S(1)} %copy-done.1, bf16[8,2,128,512]{3,2,1,0:T(8,128)(2,1)S(1)} %collective-permute-done.sib, f32[1,512]{1,0:T(1,128)S(1)} %bitcast.13, ...), custom_call_target="tpu_custom_call" | custom-call | tf_op jit(solution)/shard_map/inner_1/pallas_call | solution.py:246
  40.7 3.7 %collective-permute-done.6.refs_1_ = bf16[6,56,512]{2,1,0:T(8,128)(2,1)S(1)} collective-permute-done((bf16[6,56,512]{2,1,0:T(8,128)(2,1)S(1)}, bf16[6,56,512]{2,1,0:T(8,128)(2,1)S(1)}, u32[]{:S(2)}, u32[]{:S(2)}) %collective-permute-start.6) | collective-permute-done | bytes 344096 | tf_op jit(solution)/shard_map/ppermute | solution.py:37
  45.8 2.5 %halo_1.1 = (bf16[12,64,512]{2,1,0:T(8,128)(2,1)S(1)}, bf16[12,64,512]{2,1,0:T(8,128)(2,1)S(1)}, s32[4]{0:T(128)S(1)}) custom-call(s32[4]{0:T(128)S(1)} %get-tuple-element.97.info, f32[12,64,512]{2,1,0:T(8,128)S(1)} %get-tuple-element.98.partial, bf16[6,72,512]{2,1,0:T(8,128)(2,1)S(1)} %collective-permute-done.3.refs_0_, ...), custom_call_target="tpu_custom_call" | custom-call | tf_op jit(solution)/shard_map/halo_1/pallas_call | solution.py:308
  48.4 2.5 %temporal_1.1 = (bf16[16,64,512]{2,1,0:T(8,128)(2,1)S(1)}, bf16[1,64,512]{2,1,0:T(8,128)(2,1)S(1)}, bf16[15,48,512]{2,1,0:T(8,128)(2,1)S(1)}, bf16[15,16,512]{2,1,0:T(8,128)(2,1)S(1)}, s32[4]{0:T(128)S(1)}) custom-call(s32[4]{0:T(128)S(1)} %get-tuple-element.101.info, bf16[12,64,512]{2,1,0:T(8,128)(2,1)S(1)} %get-tuple-element.102.gated, ...), custom_call_target="tpu_custom_call" | custom-call | tf_op jit(solution)/shard_map/temporal_1/pallas_call | solution.py:376
  52.5 2.8 %project_0.1 = (bf16[8,128,512]{2,1,0:T(8,128)(2,1)S(1)}, bf16[8,128,512]{2,1,0:T(8,128)(2,1)S(1)}, bf16[8,128,512]{2,1,0:T(8,128)(2,1)S(1)}, s32[4]{0:T(128)S(1)}) custom-call(s32[4]{0:T(128)S(1)} %get-tuple-element.104.info, bf16[1,64,512]{2,1,0:T(8,128)(2,1)S(1)} %get-tuple-element.105.n_first, bf16[15,64,512]{2,1,0:T(8,128)(2,1)S(1)} %get-tuple-element.106.refs_0_, ...), custom_call_target="tpu_custom_call" | custom-call | tf_op jit(solution)/shard_map/project_0/pallas_call | solution.py:419
  55.3 2.8 %project_1.1 = (bf16[8,128,512]{2,1,0:T(8,128)(2,1)S(1)}, bf16[8,128,512]{2,1,0:T(8,128)(2,1)S(1)}, bf16[8,128,512]{2,1,0:T(8,128)(2,1)S(1)}, s32[4]{0:T(128)S(1)}) custom-call(s32[4]{0:T(128)S(1)} %get-tuple-element.107.info, bf16[1,64,512]{2,1,0:T(8,128)(2,1)S(1)} %get-tuple-element.108.n_first, bf16[15,48,512]{2,1,0:T(8,128)(2,1)S(1)} %get-tuple-element.109.refs_0_, ...), custom_call_target="tpu_custom_call" | custom-call | tf_op jit(solution)/shard_map/project_1/pallas_call | solution.py:419
  58.1 4.3 %collective-permute-start.11 = (bf16[15,16,512]{2,1,0:T(8,128)(2,1)S(1)}, bf16[15,16,512]{2,1,0:T(8,128)(2,1)S(1)}, u32[]{:S(2)}, u32[]{:S(2)}) collective-permute-start(bf16[15,16,512]{2,1,0:T(8,128)(2,1)S(1)} %collective-permute-done.10), channel_id=1, source_target_pairs={{0,24},{1,25},{2,26},{3,27},{4,28},{5,29},{6,30},{7,31},{8,0},{9,1... | collective-permute-start | bytes 737288 | tf_op jit(solution)/shard_map/ppermute | solution.py:37
  62.4 5.8 %attend_0.1 = (bf16[2,2,64,512]{3,2,1,0:T(8,128)(2,1)S(1)}, bf16[2,2,64,512]{3,2,1,0:T(8,128)(2,1)S(1)}, bf16[2,2,64,512]{3,2,1,0:T(8,128)(2,1)S(1)}, bf16[2,2,64,512]{3,2,1,0:T(8,128)(2,1)S(1)}, s32[4]{0:T(128)S(1)}) custom-call(s32[4]{0:T(128)S(1)} %get-tuple-element.111.info, bf16[15,64,512]{2,1,0:T(8,128)(2,1)S(1)} %collective-permute-done.8.refs_0_, ...), custom_call_target="tpu_custom_call" | custom-call | tf_op jit(solution)/shard_map/attend_0/pallas_call | solution.py:494
  68.7 4.1 %collective-permute-start.14 = (bf16[2,2,64,512]{3,2,1,0:T(8,128)(2,1)S(1)}, bf16[2,2,64,512]{3,2,1,0:T(8,128)(2,1)S(1)}, u32[]{:S(2)}, u32[]{:S(2)}) collective-permute-start(bf16[2,2,64,512]{3,2,1,0:T(8,128)(2,1)S(1)} %get-tuple-element.128), channel_id=1, source_target_pairs={{0,2},{1,3},{2,0},{3,1},{4,6},{5,7},{6,4},{7,5},{8,10},{9,11},{10,... | collective-permute-start | bytes 786440 | tf_op jit(solution)/shard_map/ppermute | solution.py:37
  73.4 6.0 %collective-permute-done.9.refs_0_ = bf16[15,48,512]{2,1,0:T(8,128)(2,1)S(1)} collective-permute-done((bf16[15,48,512]{2,1,0:T(8,128)(2,1)S(1)}, bf16[15,48,512]{2,1,0:T(8,128)(2,1)S(1)}, u32[]{:S(2)}, u32[]{:S(2)}) %collective-permute-start.9) | collective-permute-done | bytes 737312 | tf_op jit(solution)/shard_map/ppermute | solution.py:37
  79.4 5.7 %attend_1.1 = (bf16[2,2,64,512]{3,2,1,0:T(8,128)(2,1)S(1)}, bf16[2,2,64,512]{3,2,1,0:T(8,128)(2,1)S(1)}, bf16[2,2,64,512]{3,2,1,0:T(8,128)(2,1)S(1)}, bf16[2,2,64,512]{3,2,1,0:T(8,128)(2,1)S(1)}, s32[4]{0:T(128)S(1)}) custom-call(s32[4]{0:T(128)S(1)} %get-tuple-element.116.info, bf16[15,48,512]{2,1,0:T(8,128)(2,1)S(1)} %collective-permute-done.9.refs_0_, ...), custom_call_target="tpu_custom_call" | custom-call | tf_op jit(solution)/shard_map/attend_1/pallas_call | solution.py:494
  85.1 2.1 %collective-permute-start.16 = (bf16[2,2,64,512]{3,2,1,0:T(8,128)(2,1)S(1)}, bf16[2,2,64,512]{3,2,1,0:T(8,128)(2,1)S(1)}, u32[]{:S(2)}, u32[]{:S(2)}) collective-permute-start(bf16[2,2,64,512]{3,2,1,0:T(8,128)(2,1)S(1)} %get-tuple-element.133), channel_id=1, source_target_pairs={{0,1},{1,2},{2,3},{3,0},{4,5},{5,6},{6,7},{7,4},{8,9},{9,10},{10,1... | collective-permute-start | bytes 786440 | tf_op jit(solution)/shard_map/ppermute | solution.py:37
  87.3 2.2 %collective-permute-start.17 = (bf16[2,2,64,512]{3,2,1,0:T(8,128)(2,1)S(1)}, bf16[2,2,64,512]{3,2,1,0:T(8,128)(2,1)S(1)}, u32[]{:S(2)}, u32[]{:S(2)}) collective-permute-start(bf16[2,2,64,512]{3,2,1,0:T(8,128)(2,1)S(1)} %get-tuple-element.134), channel_id=1, source_target_pairs={{0,2},{1,3},{2,0},{3,1},{4,6},{5,7},{6,4},{7,5},{8,10},{9,11},{10,... | collective-permute-start | bytes 786440 | tf_op jit(solution)/shard_map/ppermute | solution.py:37
  92.6 5.2 %collective-permute-done.17.refs_2_ = bf16[2,2,64,512]{3,2,1,0:T(8,128)(2,1)S(1)} collective-permute-done((bf16[2,2,64,512]{3,2,1,0:T(8,128)(2,1)S(1)}, bf16[2,2,64,512]{3,2,1,0:T(8,128)(2,1)S(1)}, u32[]{:S(2)}, u32[]{:S(2)}) %collective-permute-start.17) | collective-permute-done | bytes 262176 | tf_op jit(solution)/shard_map/ppermute | solution.py:37
  97.8 4.5 %collective-permute-start.19 = (bf16[4,2,64,512]{3,2,1,0:T(8,128)(2,1)S(1)}, bf16[4,2,64,512]{3,2,1,0:T(8,128)(2,1)S(1)}, u32[]{:S(2)}, u32[]{:S(2)}) collective-permute-start(bf16[4,2,64,512]{3,2,1,0:T(8,128)(2,1)S(1)} %get-tuple-element.140), channel_id=1, source_target_pairs={{0,4},{1,5},{2,6},{3,7},{4,0},{5,1},{6,2},{7,3},{8,12},{9,13},{10,... | collective-permute-start | bytes 1572872 | tf_op jit(solution)/shard_map/ppermute | solution.py:37
  103.9 2.2 %place_0.1 = (bf16[2,8,128,512]{3,2,1,0:T(8,128)(2,1)}, s32[4]{0:T(128)S(1)}) custom-call(s32[4]{0:T(128)S(1)} %get-tuple-element.139.info, bf16[2,2,64,512]{3,2,1,0:T(8,128)(2,1)S(1)} %get-tuple-element.126.refs_0_, bf16[2,2,64,512]{3,2,1,0:T(8,128)(2,1)S(1)} %collective-permute-done.13.refs_1_, ...), custom_call_target="tpu_custom_call" | custom-call | tf_op jit(solution)/shard_map/place_0/pallas_call | solution.py:551
  (59 shorter events, 23.0 us)
Async XLA Ops:
  0.0 16.4 %collective-permute-start = (bf16[8,2,128,512]{3,2,1,0:T(8,128)(2,1)}, bf16[8,2,128,512]{3,2,1,0:T(8,128)(2,1)S(1)}, u32[]{:S(2)}, u32[]{:S(2)}) collective-permute-start(bf16[8,2,128,512]{3,2,1,0:T(8,128)(2,1)} %own.5), channel_id=1, source_target_pairs={{0,4},{1,5},{2,6},{3,7},{4,0},{5,1},{6,2},{7,3},{8,12},{9,13},{10,... | collective-permute-start | bytes 6291464 | tf_op jit(solution)/shard_map/ppermute | solution.py:37
  4.2 8.0 %collective-permute-start.1 = (bf16[2,128,512]{2,1,0:T(8,128)(2,1)S(1)}, bf16[2,128,512]{2,1,0:T(8,128)(2,1)S(1)}, u32[]{:S(2)}, u32[]{:S(2)}) collective-permute-start(bf16[2,128,512]{2,1,0:T(8,128)(2,1)S(1)} %get-tuple-element.81), channel_id=1, source_target_pairs={{0,1},{1,2},{2,3},{3,0},{4,7},{5,4},{6,5},{7,6},{8,9},{9,10},{10,1... | collective-permute-start | bytes 786440 | tf_op jit(solution)/shard_map/ppermute | solution.py:37
  7.1 6.1 %collective-permute-start.2 = (bf16[2,128,512]{2,1,0:T(8,128)(2,1)S(1)}, bf16[2,128,512]{2,1,0:T(8,128)(2,1)S(1)}, u32[]{:S(2)}, u32[]{:S(2)}) collective-permute-start(bf16[2,128,512]{2,1,0:T(8,128)(2,1)S(1)} %get-tuple-element.82), channel_id=1, source_target_pairs={{0,7},{1,4},{2,5},{3,6},{4,1},{5,2},{6,3},{7,0},{8,15},{9,12},{10,... | collective-permute-start | bytes 786440 | tf_op jit(solution)/shard_map/ppermute | solution.py:37
  9.5 6.9 %copy-start.8 = (f32[512]{0:T(512)S(1)}, f32[512]{0:T(512)}, u32[]{:S(2)}) copy-start(f32[512]{0:T(512)} %param.11) | copy-start | bytes 6148
  9.5 6.9 %copy-start.9 = (f32[512]{0:T(512)S(1)}, f32[512]{0:T(512)}, u32[]{:S(2)}) copy-start(f32[512]{0:T(512)} %param.13) | copy-start | bytes 6148
  13.2 12.6 %collective-permute-start.3 = (bf16[6,72,512]{2,1,0:T(8,128)(2,1)S(1)}, bf16[6,72,512]{2,1,0:T(8,128)(2,1)S(1)}, u32[]{:S(2)}, u32[]{:S(2)}) collective-permute-start(bf16[6,72,512]{2,1,0:T(8,128)(2,1)S(1)} %get-tuple-element.89), channel_id=1, source_target_pairs={{0,1},{1,2},{2,3},{3,0},{4,7},{5,4},{6,5},{7,6},{8,9},{9,10},{10,1... | collective-permute-start | bytes 1327112 | tf_op jit(solution)/shard_map/ppermute | solution.py:37
  16.4 9.4 %collective-permute-start.4 = (bf16[6,72,512]{2,1,0:T(8,128)(2,1)S(1)}, bf16[6,72,512]{2,1,0:T(8,128)(2,1)S(1)}, u32[]{:S(2)}, u32[]{:S(2)}) collective-permute-start(bf16[6,72,512]{2,1,0:T(8,128)(2,1)S(1)} %get-tuple-element.90), channel_id=1, source_target_pairs={{0,7},{1,4},{2,5},{3,6},{4,1},{5,2},{6,3},{7,0},{8,15},{9,12},{10,... | collective-permute-start | bytes 1327112 | tf_op jit(solution)/shard_map/ppermute | solution.py:37
  20.2 12.4 %collective-permute-start.5 = (bf16[2,128,512]{2,1,0:T(8,128)(2,1)S(1)}, bf16[2,128,512]{2,1,0:T(8,128)(2,1)S(1)}, u32[]{:S(2)}, u32[]{:S(2)}) collective-permute-start(bf16[2,128,512]{2,1,0:T(8,128)(2,1)S(1)} %slice.3), channel_id=1, source_target_pairs={{0,8},{1,9},{2,10},{3,11},{4,12},{5,13},{6,14},{7,15},{8,16},{9,17... | collective-permute-start | bytes 786440 | tf_op jit(solution)/shard_map/ppermute | solution.py:37
  35.6 26.9 %collective-permute-start.8 = (bf16[15,64,512]{2,1,0:T(8,128)(2,1)S(1)}, bf16[15,64,512]{2,1,0:T(8,128)(2,1)S(1)}, u32[]{:S(2)}, u32[]{:S(2)}) collective-permute-start(bf16[15,64,512]{2,1,0:T(8,128)(2,1)S(1)} %get-tuple-element.106.refs_0_), channel_id=1, source_target_pairs={{0,8},{1,9},{2,10},{3,11},{4,12},{5,13},{6,14},{7,15},{8,16},{9,17... | collective-permute-start | bytes 2949128 | tf_op jit(solution)/shard_map/ppermute | solution.py:37
  35.6 8.8 %collective-permute-start.6 = (bf16[6,56,512]{2,1,0:T(8,128)(2,1)S(1)}, bf16[6,56,512]{2,1,0:T(8,128)(2,1)S(1)}, u32[]{:S(2)}, u32[]{:S(2)}) collective-permute-start(bf16[6,56,512]{2,1,0:T(8,128)(2,1)S(1)} %get-tuple-element.99), channel_id=1, source_target_pairs={{0,1},{1,2},{2,3},{3,0},{4,7},{5,4},{6,5},{7,6},{8,9},{9,10},{10,1... | collective-permute-start | bytes 1032200 | tf_op jit(solution)/shard_map/ppermute | solution.py:37
  37.4 8.4 %collective-permute-start.7 = (bf16[6,56,512]{2,1,0:T(8,128)(2,1)S(1)}, bf16[6,56,512]{2,1,0:T(8,128)(2,1)S(1)}, u32[]{:S(2)}, u32[]{:S(2)}) collective-permute-start(bf16[6,56,512]{2,1,0:T(8,128)(2,1)S(1)} %get-tuple-element.100), channel_id=1, source_target_pairs={{0,7},{1,4},{2,5},{3,6},{4,1},{5,2},{6,3},{7,0},{8,15},{9,12},{10,... | collective-permute-start | bytes 1032200 | tf_op jit(solution)/shard_map/ppermute | solution.py:37
  50.9 7.2 %collective-permute-start.10 = (bf16[15,16,512]{2,1,0:T(8,128)(2,1)S(1)}, bf16[15,16,512]{2,1,0:T(8,128)(2,1)S(1)}, u32[]{:S(2)}, u32[]{:S(2)}) collective-permute-start(bf16[15,16,512]{2,1,0:T(8,128)(2,1)S(1)} %get-tuple-element.110.refs_1_), channel_id=1, source_target_pairs={{0,24},{1,25},{2,26},{3,27},{4,28},{5,29},{6,30},{7,31},{8,0},{9,1... | collective-permute-start | bytes 737288 | tf_op jit(solution)/shard_map/ppermute | solution.py:37
  52.4 27.0 %collective-permute-start.9 = (bf16[15,48,512]{2,1,0:T(8,128)(2,1)S(1)}, bf16[15,48,512]{2,1,0:T(8,128)(2,1)S(1)}, u32[]{:S(2)}, u32[]{:S(2)}) collective-permute-start(bf16[15,48,512]{2,1,0:T(8,128)(2,1)S(1)} %get-tuple-element.109.refs_0_), channel_id=1, source_target_pairs={{0,8},{1,9},{2,10},{3,11},{4,12},{5,13},{6,14},{7,15},{8,16},{9,17... | collective-permute-start | bytes 2211848 | tf_op jit(solution)/shard_map/ppermute | solution.py:37
  52.4 10.0 %copy-start.7 = (bf16[512,512]{1,0:T(8,128)(2,1)S(1)}, bf16[512,512]{1,0:T(8,128)(2,1)}, u32[]{:S(2)}) copy-start(bf16[512,512]{1,0:T(8,128)(2,1)} %refs_4_.3) | copy-start | bytes 1572868
  58.1 10.5 %collective-permute-start.11 = (bf16[15,16,512]{2,1,0:T(8,128)(2,1)S(1)}, bf16[15,16,512]{2,1,0:T(8,128)(2,1)S(1)}, u32[]{:S(2)}, u32[]{:S(2)}) collective-permute-start(bf16[15,16,512]{2,1,0:T(8,128)(2,1)S(1)} %collective-permute-done.10), channel_id=1, source_target_pairs={{0,24},{1,25},{2,26},{3,27},{4,28},{5,29},{6,30},{7,31},{8,0},{9,1... | collective-permute-start | bytes 737288 | tf_op jit(solution)/shard_map/ppermute | solution.py:37
  68.3 21.2 %collective-permute-start.13 = (bf16[2,2,64,512]{3,2,1,0:T(8,128)(2,1)S(1)}, bf16[2,2,64,512]{3,2,1,0:T(8,128)(2,1)S(1)}, u32[]{:S(2)}, u32[]{:S(2)}) collective-permute-start(bf16[2,2,64,512]{3,2,1,0:T(8,128)(2,1)S(1)} %get-tuple-element.127), channel_id=1, source_target_pairs={{0,1},{1,2},{2,3},{3,0},{4,5},{5,6},{6,7},{7,4},{8,9},{9,10},{10,1... | collective-permute-start | bytes 786440 | tf_op jit(solution)/shard_map/ppermute | solution.py:37
  68.6 10.8 %collective-permute-start.12 = (bf16[15,16,512]{2,1,0:T(8,128)(2,1)S(1)}, bf16[15,16,512]{2,1,0:T(8,128)(2,1)S(1)}, u32[]{:S(2)}, u32[]{:S(2)}) collective-permute-start(bf16[15,16,512]{2,1,0:T(8,128)(2,1)S(1)} %collective-permute-done.11), channel_id=1, source_target_pairs={{0,24},{1,25},{2,26},{3,27},{4,28},{5,29},{6,30},{7,31},{8,32},{9,... | collective-permute-start | bytes 737288 | tf_op jit(solution)/shard_map/ppermute | solution.py:37
  68.7 22.8 %collective-permute-start.14 = (bf16[2,2,64,512]{3,2,1,0:T(8,128)(2,1)S(1)}, bf16[2,2,64,512]{3,2,1,0:T(8,128)(2,1)S(1)}, u32[]{:S(2)}, u32[]{:S(2)}) collective-permute-start(bf16[2,2,64,512]{3,2,1,0:T(8,128)(2,1)S(1)} %get-tuple-element.128), channel_id=1, source_target_pairs={{0,2},{1,3},{2,0},{3,1},{4,6},{5,7},{6,4},{7,5},{8,10},{9,11},{10,... | collective-permute-start | bytes 786440 | tf_op jit(solution)/shard_map/ppermute | solution.py:37
  72.7 18.7 %collective-permute-start.15 = (bf16[2,2,64,512]{3,2,1,0:T(8,128)(2,1)S(1)}, bf16[2,2,64,512]{3,2,1,0:T(8,128)(2,1)S(1)}, u32[]{:S(2)}, u32[]{:S(2)}) collective-permute-start(bf16[2,2,64,512]{3,2,1,0:T(8,128)(2,1)S(1)} %get-tuple-element.129), channel_id=1, source_target_pairs={{0,3},{1,0},{2,1},{3,2},{4,7},{5,4},{6,5},{7,6},{8,11},{9,8},{10,9... | collective-permute-start | bytes 786440 | tf_op jit(solution)/shard_map/ppermute | solution.py:37
  85.1 7.5 %collective-permute-start.16 = (bf16[2,2,64,512]{3,2,1,0:T(8,128)(2,1)S(1)}, bf16[2,2,64,512]{3,2,1,0:T(8,128)(2,1)S(1)}, u32[]{:S(2)}, u32[]{:S(2)}) collective-permute-start(bf16[2,2,64,512]{3,2,1,0:T(8,128)(2,1)S(1)} %get-tuple-element.133), channel_id=1, source_target_pairs={{0,1},{1,2},{2,3},{3,0},{4,5},{5,6},{6,7},{7,4},{8,9},{9,10},{10,1... | collective-permute-start | bytes 786440 | tf_op jit(solution)/shard_map/ppermute | solution.py:37
  87.3 10.5 %collective-permute-start.17 = (bf16[2,2,64,512]{3,2,1,0:T(8,128)(2,1)S(1)}, bf16[2,2,64,512]{3,2,1,0:T(8,128)(2,1)S(1)}, u32[]{:S(2)}, u32[]{:S(2)}) collective-permute-start(bf16[2,2,64,512]{3,2,1,0:T(8,128)(2,1)S(1)} %get-tuple-element.134), channel_id=1, source_target_pairs={{0,2},{1,3},{2,0},{3,1},{4,6},{5,7},{6,4},{7,5},{8,10},{9,11},{10,... | collective-permute-start | bytes 786440 | tf_op jit(solution)/shard_map/ppermute | solution.py:37
  89.5 8.3 %collective-permute-start.18 = (bf16[2,2,64,512]{3,2,1,0:T(8,128)(2,1)S(1)}, bf16[2,2,64,512]{3,2,1,0:T(8,128)(2,1)S(1)}, u32[]{:S(2)}, u32[]{:S(2)}) collective-permute-start(bf16[2,2,64,512]{3,2,1,0:T(8,128)(2,1)S(1)} %get-tuple-element.135), channel_id=1, source_target_pairs={{0,3},{1,0},{2,1},{3,2},{4,7},{5,4},{6,5},{7,6},{8,11},{9,8},{10,9... | collective-permute-start | bytes 786440 | tf_op jit(solution)/shard_map/ppermute | solution.py:37
  97.8 6.1 %collective-permute-start.19 = (bf16[4,2,64,512]{3,2,1,0:T(8,128)(2,1)S(1)}, bf16[4,2,64,512]{3,2,1,0:T(8,128)(2,1)S(1)}, u32[]{:S(2)}, u32[]{:S(2)}) collective-permute-start(bf16[4,2,64,512]{3,2,1,0:T(8,128)(2,1)S(1)} %get-tuple-element.140), channel_id=1, source_target_pairs={{0,4},{1,5},{2,6},{3,7},{4,0},{5,1},{6,2},{7,3},{8,12},{9,13},{10,... | collective-permute-start | bytes 1572872 | tf_op jit(solution)/shard_map/ppermute | solution.py:37
  103.5 2.6 %collective-permute-start.20 = (bf16[4,2,64,512]{3,2,1,0:T(8,128)(2,1)S(1)}, bf16[4,2,64,512]{3,2,1,0:T(8,128)(2,1)S(1)}, u32[]{:S(2)}, u32[]{:S(2)}) collective-permute-start(bf16[4,2,64,512]{3,2,1,0:T(8,128)(2,1)S(1)} %get-tuple-element.142), channel_id=1, source_target_pairs={{0,4},{1,5},{2,6},{3,7},{4,0},{5,1},{6,2},{7,3},{8,12},{9,13},{10,... | collective-permute-start | bytes 1572872 | tf_op jit(solution)/shard_map/ppermute | solution.py:37
  (8 other events, 33.8 us)

commit v3 on v2

--- a/solution.py
+++ b/solution.py
@@ -17,7 +17,7 @@
 MAIN = 8 - EDGE
 CUTS = (0, 64, 128)
 RING = 16
-ORDER = ("e0", "i0", "s0", "t0", "i1", "s1", "t1", "p0", "p1", "a0", "a1", "d0", "d1", "w0", "w1")
+ORDER = ("e0", "i0", "s0", "t0", "i1", "s1", "t1", "p0", "p1", "a0", "a1", "d0", "d1", "w0")
 AXES = ("frames", "rows")
 F32 = jnp.float32
 BF16 = jnp.bfloat16
@@ -529,36 +529,36 @@
     )(info, *blocks)
 
 
-def place_kernel(j, info, *refs):
-    blocks, got, (out, info_out, sems) = refs[:4], refs[4], refs[-3:]
-    pass_on(info, info_out)
-    c0, c1 = CUTS[j], CUTS[j + 1]
+def place_kernel(info, *refs):
+    blocks, (out, info_out, sems) = refs[:-3], refs[-3:]
+    pass_on(info, info_out)
     core, band = info[0], info[3]
     copies = []
-    for n in range(4):
-        row = 2 * lax.rem(band + 4 - n, 4)
-        for i, (src, at) in enumerate(((blocks[n].at[0], core), (got.at[n], 1 - core))):
-            dst = out.at[:, row + at, c0:c1, :]
-            copies.append(pltpu.make_async_copy(src, dst, sems.at[2 * n + i]))
+    for j in range(len(CUTS) - 1):
+        c0, c1 = CUTS[j], CUTS[j + 1]
+        *kept, got = blocks[5 * j : 5 * j + 5]
+        for n in range(4):
+            row = 2 * lax.rem(band + 4 - n, 4)
+            for src, at in ((kept[n].at[0], core), (got.at[n], 1 - core)):
+                dst = out.at[:, row + at, c0:c1, :]
+                copies.append(pltpu.make_async_copy(src, dst, sems.at[len(copies)]))
     for copy in copies:
         copy.start()
     for copy in copies:
         copy.wait()
 
 
-def place_stage(j, info, blocks, got, whole):
-    earlier = () if whole is None else (whole,)
-    return pl.pallas_call(
-        functools.partial(place_kernel, j),
+def place_stage(info, blocks):
+    return pl.pallas_call(
+        place_kernel,
         out_shape=(jax.ShapeDtypeStruct((2, 8, W, C), BF16), INFO),
-        in_specs=[SMEM] + [VMEM] * 5 + [HBM] * len(earlier),
+        in_specs=[SMEM] + [VMEM] * len(blocks),
         out_specs=(HBM, SMEM),
-        scratch_shapes=[pltpu.SemaphoreType.DMA((8,))],
-        input_output_aliases={6: 0} if earlier else {},
+        scratch_shapes=[pltpu.SemaphoreType.DMA((8 * (len(CUTS) - 1),))],
         compiler_params=pltpu.CompilerParams(vmem_limit_bytes=8 * 2**20),
         cost_estimate=LIGHT,
-        name=f"place_{j}",
-    )(info, *blocks, got, *earlier)
+        name="place",
+    )(info, *blocks)
 
 
 def shards(
@@ -673,8 +673,8 @@
         return info
 
     def place(j, info):
-        s = state[j]
-        shared["out"], info = place_stage(j, info, s["blocks"], s["got"], shared.get("out"))
+        blocks = [block for s in state for block in (*s["blocks"], s["got"])]
+        shared["out"], info = place_stage(info, blocks)
         return info
 
     stages = {

time: 109 us -> 109 us (level)
  waiting for transfers between devices: 24 us -> 25.9 us
  Pallas kernels: 47.3 us -> 45.5 us
    ppermute x21, waiting for transfers between devices: 24 us -> 25.9 us  [routed(): return lax.ppermute(x, AXES, pairs)]
    pallas_call x2 -> x1, Pallas kernels: 4.26 us -> 2.5 us  [place_stage(): pl.pallas_call(place_kernel, out_shape=(jax.ShapeDtypeStruct((2, 8, W, C)...]
  transfers between devices with their start and end apart: 21 -> 21, of which waited for: 9 -> 10; matrix products, arithmetic and copies ran while one was open for 0% -> 0% of each run, Pallas kernels for 39% -> 36%
where the time goes in v3:
time: 109 us
  Pallas kernels  45.5 us (42%)
  starting transfers between devices  32.7 us (30%)
  waiting for transfers between devices  25.9 us (24%)
  local copies, waits for them, and re-layouts  3.99 us (4%)
    ppermute x21, starting transfers between devices, routed(): return lax.ppermute(x, AXES, pairs)  32.7 us
    ppermute x21, waiting for transfers between devices, routed(): return lax.ppermute(x, AXES, pairs)  25.9 us
    pallas_call x2, Pallas kernels, attend_stage(): pl.pallas_call(functools.partial(attend_kernel, wc, len(ctx)), out_shape=...  11.5 us
    pallas_call x2, Pallas kernels, inner_stage(): pl.pallas_call(functools.partial(inner_kernel, j), out_shape=(jax.ShapeDt...  6.53 us
    pallas_call x2, Pallas kernels, qkv_stage(): pl.pallas_call(functools.partial(qkv_kernel, wc, len(n_rest)), out_shape=...  5.62 us
    pallas_call x2, Pallas kernels, temporal_stage(): pl.pallas_call(functools.partial(temporal_kernel, j), out_shape=(jax.Shap...  5.48 us
    pallas_call x2, Pallas kernels, halo_stage(): pl.pallas_call(functools.partial(halo_kernel, j, n), out_shape=(shape, sh...  5.08 us
    unnamed x22, local copies, waits for them, and re-layouts  3.97 us
  transfers between devices with their start and end apart: 21, of which 10 were waited for; matrix products, arithmetic and copies ran while one was open for 0% of the time, Pallas kernels for 36%

profile of v3, /device:TPU:1, one launch (start us, length us, event | category | flops | bytes accessed | tf_op | source)
XLA Modules:
  0.0 108.5 jit_solution(11054733386407823567)
XLA Ops:
  4.2 2.9 %collective-permute-start.1 = (bf16[2,128,512]{2,1,0:T(8,128)(2,1)S(1)}, bf16[2,128,512]{2,1,0:T(8,128)(2,1)S(1)}, u32[]{:S(2)}, u32[]{:S(2)}) collective-permute-start(bf16[2,128,512]{2,1,0:T(8,128)(2,1)S(1)} %get-tuple-element.79), channel_id=1, source_target_pairs={{0,1},{1,2},{2,3},{3,0},{4,7},{5,4},{6,5},{7,6},{8,9},{9,10},{10,1... | collective-permute-start | bytes 786440 | tf_op jit(solution)/shard_map/ppermute | solution.py:37
  7.2 2.3 %copy-done.5 = bf16[3,3,512,512]{3,2,1,0:T(8,128)(2,1)S(1)} copy-done((bf16[3,3,512,512]{3,2,1,0:T(8,128)(2,1)S(1)}, bf16[3,3,512,512]{3,2,1,0:T(8,128)(2,1)}, u32[]{:S(2)}) %copy-start.5) | copy-done | bytes 4718616
  13.2 3.1 %collective-permute-start.3 = (bf16[6,72,512]{2,1,0:T(8,128)(2,1)S(1)}, bf16[6,72,512]{2,1,0:T(8,128)(2,1)S(1)}, u32[]{:S(2)}, u32[]{:S(2)}) collective-permute-start(bf16[6,72,512]{2,1,0:T(8,128)(2,1)S(1)} %get-tuple-element.87), channel_id=1, source_target_pairs={{0,1},{1,2},{2,3},{3,0},{4,7},{5,4},{6,5},{7,6},{8,9},{9,10},{10,1... | collective-permute-start | bytes 1327112 | tf_op jit(solution)/shard_map/ppermute | solution.py:37
  16.4 3.8 %edge.1 = (bf16[4,128,512]{2,1,0:T(8,128)(2,1)S(1)}, bf16[4,128,512]{2,1,0:T(8,128)(2,1)S(1)}, s32[4]{0:T(128)S(1)}) custom-call(s32[4]{0:T(128)S(1)} %get-tuple-element.74.info, bf16[8,2,128,512]{3,2,1,0:T(8,128)(2,1)S(1)} %copy-done.1, bf16[8,2,128,512]{3,2,1,0:T(8,128)(2,1)S(1)} %collective-permute-done.sib, ...), custom_call_target="tpu_custom_call" | custom-call | tf_op jit(solution)/shard_map/edge/pallas_call | solution.py:204
  21.5 3.3 %inner_0.1 = (f32[12,64,512]{2,1,0:T(8,128)S(1)}, s32[4]{0:T(128)S(1)}) custom-call(s32[4]{0:T(128)S(1)} %get-tuple-element.84.info, bf16[8,2,128,512]{3,2,1,0:T(8,128)(2,1)S(1)} %copy-done.1, bf16[8,2,128,512]{3,2,1,0:T(8,128)(2,1)S(1)} %collective-permute-done.sib, f32[1,512]{1,0:T(1,128)S(1)} %bitcast.11, ...), custom_call_target="tpu_custom_call" | custom-call | tf_op jit(solution)/shard_map/inner_0/pallas_call | solution.py:246
  25.8 2.5 %halo_0.1 = (bf16[12,64,512]{2,1,0:T(8,128)(2,1)S(1)}, bf16[12,64,512]{2,1,0:T(8,128)(2,1)S(1)}, s32[4]{0:T(128)S(1)}) custom-call(s32[4]{0:T(128)S(1)} %get-tuple-element.85.info, f32[12,64,512]{2,1,0:T(8,128)S(1)} %get-tuple-element.86.partial, bf16[6,72,512]{2,1,0:T(8,128)(2,1)S(1)} %collective-permute-done.3.refs_0_, ...), custom_call_target="tpu_custom_call" | custom-call | tf_op jit(solution)/shard_map/halo_0/pallas_call | solution.py:308
  28.4 4.2 %collective-permute-done.5.before = bf16[2,128,512]{2,1,0:T(8,128)(2,1)S(1)} collective-permute-done((bf16[2,128,512]{2,1,0:T(8,128)(2,1)S(1)}, bf16[2,128,512]{2,1,0:T(8,128)(2,1)S(1)}, u32[]{:S(2)}, u32[]{:S(2)}) %collective-permute-start.5) | collective-permute-done | bytes 262176 | tf_op jit(solution)/shard_map/ppermute | solution.py:37
  32.6 3.0 %temporal_0.1 = (bf16[16,64,512]{2,1,0:T(8,128)(2,1)S(1)}, bf16[1,64,512]{2,1,0:T(8,128)(2,1)S(1)}, bf16[15,64,512]{2,1,0:T(8,128)(2,1)S(1)}, s32[4]{0:T(128)S(1)}) custom-call(s32[4]{0:T(128)S(1)} %get-tuple-element.89.info, bf16[12,64,512]{2,1,0:T(8,128)(2,1)S(1)} %get-tuple-element.90.gated, bf16[4,128,512]{2,1,0:T(8,128)(2,1)S(1)} %get-tuple-element.91.edge_gated, ...), custom_call_target="tpu_custom_call" | custom-call | tf_op jit(solution)/shard_map/temporal_0/pallas_call | solution.py:376
  37.4 3.3 %inner_1.1 = (f32[12,64,512]{2,1,0:T(8,128)S(1)}, s32[4]{0:T(128)S(1)}) custom-call(s32[4]{0:T(128)S(1)} %get-tuple-element.94.info, bf16[8,2,128,512]{3,2,1,0:T(8,128)(2,1)S(1)} %copy-done.1, bf16[8,2,128,512]{3,2,1,0:T(8,128)(2,1)S(1)} %collective-permute-done.sib, f32[1,512]{1,0:T(1,128)S(1)} %bitcast.13, ...), custom_call_target="tpu_custom_call" | custom-call | tf_op jit(solution)/shard_map/inner_1/pallas_call | solution.py:246
  40.7 3.7 %collective-permute-done.6.refs_1_ = bf16[6,56,512]{2,1,0:T(8,128)(2,1)S(1)} collective-permute-done((bf16[6,56,512]{2,1,0:T(8,128)(2,1)S(1)}, bf16[6,56,512]{2,1,0:T(8,128)(2,1)S(1)}, u32[]{:S(2)}, u32[]{:S(2)}) %collective-permute-start.6) | collective-permute-done | bytes 344096 | tf_op jit(solution)/shard_map/ppermute | solution.py:37
  45.8 2.5 %halo_1.1 = (bf16[12,64,512]{2,1,0:T(8,128)(2,1)S(1)}, bf16[12,64,512]{2,1,0:T(8,128)(2,1)S(1)}, s32[4]{0:T(128)S(1)}) custom-call(s32[4]{0:T(128)S(1)} %get-tuple-element.95.info, f32[12,64,512]{2,1,0:T(8,128)S(1)} %get-tuple-element.96.partial, bf16[6,72,512]{2,1,0:T(8,128)(2,1)S(1)} %collective-permute-done.3.refs_0_, ...), custom_call_target="tpu_custom_call" | custom-call | tf_op jit(solution)/shard_map/halo_1/pallas_call | solution.py:308
  48.4 2.5 %temporal_1.1 = (bf16[16,64,512]{2,1,0:T(8,128)(2,1)S(1)}, bf16[1,64,512]{2,1,0:T(8,128)(2,1)S(1)}, bf16[15,48,512]{2,1,0:T(8,128)(2,1)S(1)}, bf16[15,16,512]{2,1,0:T(8,128)(2,1)S(1)}, s32[4]{0:T(128)S(1)}) custom-call(s32[4]{0:T(128)S(1)} %get-tuple-element.99.info, bf16[12,64,512]{2,1,0:T(8,128)(2,1)S(1)} %get-tuple-element.100.gated, ...), custom_call_target="tpu_custom_call" | custom-call | tf_op jit(solution)/shard_map/temporal_1/pallas_call | solution.py:376
  52.5 2.8 %project_0.1 = (bf16[8,128,512]{2,1,0:T(8,128)(2,1)S(1)}, bf16[8,128,512]{2,1,0:T(8,128)(2,1)S(1)}, bf16[8,128,512]{2,1,0:T(8,128)(2,1)S(1)}, s32[4]{0:T(128)S(1)}) custom-call(s32[4]{0:T(128)S(1)} %get-tuple-element.102.info, bf16[1,64,512]{2,1,0:T(8,128)(2,1)S(1)} %get-tuple-element.103.n_first, bf16[15,64,512]{2,1,0:T(8,128)(2,1)S(1)} %get-tuple-element.104.refs_0_, ...), custom_call_target="tpu_custom_call" | custom-call | tf_op jit(solution)/shard_map/project_0/pallas_call | solution.py:419
  55.3 2.8 %project_1.1 = (bf16[8,128,512]{2,1,0:T(8,128)(2,1)S(1)}, bf16[8,128,512]{2,1,0:T(8,128)(2,1)S(1)}, bf16[8,128,512]{2,1,0:T(8,128)(2,1)S(1)}, s32[4]{0:T(128)S(1)}) custom-call(s32[4]{0:T(128)S(1)} %get-tuple-element.105.info, bf16[1,64,512]{2,1,0:T(8,128)(2,1)S(1)} %get-tuple-element.106.n_first, bf16[15,48,512]{2,1,0:T(8,128)(2,1)S(1)} %get-tuple-element.107.refs_0_, ...), custom_call_target="tpu_custom_call" | custom-call | tf_op jit(solution)/shard_map/project_1/pallas_call | solution.py:419
  58.1 4.3 %collective-permute-start.11 = (bf16[15,16,512]{2,1,0:T(8,128)(2,1)S(1)}, bf16[15,16,512]{2,1,0:T(8,128)(2,1)S(1)}, u32[]{:S(2)}, u32[]{:S(2)}) collective-permute-start(bf16[15,16,512]{2,1,0:T(8,128)(2,1)S(1)} %collective-permute-done.10), channel_id=1, source_target_pairs={{0,24},{1,25},{2,26},{3,27},{4,28},{5,29},{6,30},{7,31},{8,0},{9,1... | collective-permute-start | bytes 737288 | tf_op jit(solution)/shard_map/ppermute | solution.py:37
  62.4 5.8 %attend_0.1 = (bf16[2,2,64,512]{3,2,1,0:T(8,128)(2,1)S(1)}, bf16[2,2,64,512]{3,2,1,0:T(8,128)(2,1)S(1)}, bf16[2,2,64,512]{3,2,1,0:T(8,128)(2,1)S(1)}, bf16[2,2,64,512]{3,2,1,0:T(8,128)(2,1)S(1)}, s32[4]{0:T(128)S(1)}) custom-call(s32[4]{0:T(128)S(1)} %get-tuple-element.109.info, bf16[15,64,512]{2,1,0:T(8,128)(2,1)S(1)} %collective-permute-done.8.refs_0_, ...), custom_call_target="tpu_custom_call" | custom-call | tf_op jit(solution)/shard_map/attend_0/pallas_call | solution.py:494
  68.7 4.1 %collective-permute-start.14 = (bf16[2,2,64,512]{3,2,1,0:T(8,128)(2,1)S(1)}, bf16[2,2,64,512]{3,2,1,0:T(8,128)(2,1)S(1)}, u32[]{:S(2)}, u32[]{:S(2)}) collective-permute-start(bf16[2,2,64,512]{3,2,1,0:T(8,128)(2,1)S(1)} %get-tuple-element.126), channel_id=1, source_target_pairs={{0,2},{1,3},{2,0},{3,1},{4,6},{5,7},{6,4},{7,5},{8,10},{9,11},{10,... | collective-permute-start | bytes 786440 | tf_op jit(solution)/shard_map/ppermute | solution.py:37
  73.4 6.0 %collective-permute-done.9.refs_0_ = bf16[15,48,512]{2,1,0:T(8,128)(2,1)S(1)} collective-permute-done((bf16[15,48,512]{2,1,0:T(8,128)(2,1)S(1)}, bf16[15,48,512]{2,1,0:T(8,128)(2,1)S(1)}, u32[]{:S(2)}, u32[]{:S(2)}) %collective-permute-start.9) | collective-permute-done | bytes 737312 | tf_op jit(solution)/shard_map/ppermute | solution.py:37
  79.4 5.7 %attend_1.1 = (bf16[2,2,64,512]{3,2,1,0:T(8,128)(2,1)S(1)}, bf16[2,2,64,512]{3,2,1,0:T(8,128)(2,1)S(1)}, bf16[2,2,64,512]{3,2,1,0:T(8,128)(2,1)S(1)}, bf16[2,2,64,512]{3,2,1,0:T(8,128)(2,1)S(1)}, s32[4]{0:T(128)S(1)}) custom-call(s32[4]{0:T(128)S(1)} %get-tuple-element.114.info, bf16[15,48,512]{2,1,0:T(8,128)(2,1)S(1)} %collective-permute-done.9.refs_0_, ...), custom_call_target="tpu_custom_call" | custom-call | tf_op jit(solution)/shard_map/attend_1/pallas_call | solution.py:494
  85.1 2.1 %collective-permute-start.16 = (bf16[2,2,64,512]{3,2,1,0:T(8,128)(2,1)S(1)}, bf16[2,2,64,512]{3,2,1,0:T(8,128)(2,1)S(1)}, u32[]{:S(2)}, u32[]{:S(2)}) collective-permute-start(bf16[2,2,64,512]{3,2,1,0:T(8,128)(2,1)S(1)} %get-tuple-element.131), channel_id=1, source_target_pairs={{0,1},{1,2},{2,3},{3,0},{4,5},{5,6},{6,7},{7,4},{8,9},{9,10},{10,1... | collective-permute-start | bytes 786440 | tf_op jit(solution)/shard_map/ppermute | solution.py:37
  87.3 2.2 %collective-permute-start.17 = (bf16[2,2,64,512]{3,2,1,0:T(8,128)(2,1)S(1)}, bf16[2,2,64,512]{3,2,1,0:T(8,128)(2,1)S(1)}, u32[]{:S(2)}, u32[]{:S(2)}) collective-permute-start(bf16[2,2,64,512]{3,2,1,0:T(8,128)(2,1)S(1)} %get-tuple-element.132), channel_id=1, source_target_pairs={{0,2},{1,3},{2,0},{3,1},{4,6},{5,7},{6,4},{7,5},{8,10},{9,11},{10,... | collective-permute-start | bytes 786440 | tf_op jit(solution)/shard_map/ppermute | solution.py:37
  92.6 5.2 %collective-permute-done.17.refs_2_.refs_7_ = bf16[2,2,64,512]{3,2,1,0:T(8,128)(2,1)S(1)} collective-permute-done((bf16[2,2,64,512]{3,2,1,0:T(8,128)(2,1)S(1)}, bf16[2,2,64,512]{3,2,1,0:T(8,128)(2,1)S(1)}, u32[]{:S(2)}, u32[]{:S(2)}) %collective-permute-start.17) | collective-permute-done | bytes 262176 | tf_op jit(solution)/shard_map/ppermute | solution.py:37
  99.0 4.6 %collective-permute-start.20 = (bf16[4,2,64,512]{3,2,1,0:T(8,128)(2,1)S(1)}, bf16[4,2,64,512]{3,2,1,0:T(8,128)(2,1)S(1)}, u32[]{:S(2)}, u32[]{:S(2)}) collective-permute-start(bf16[4,2,64,512]{3,2,1,0:T(8,128)(2,1)S(1)} %get-tuple-element.139), channel_id=1, source_target_pairs={{0,4},{1,5},{2,6},{3,7},{4,0},{5,1},{6,2},{7,3},{8,12},{9,13},{10,... | collective-permute-start | bytes 1572872 | tf_op jit(solution)/shard_map/ppermute | solution.py:37
  105.9 2.5 %place.1 = (bf16[2,8,128,512]{3,2,1,0:T(8,128)(2,1)}, s32[4]{0:T(128)}) custom-call(s32[4]{0:T(128)S(1)} %get-tuple-element.137.info, bf16[2,2,64,512]{3,2,1,0:T(8,128)(2,1)S(1)} %get-tuple-element.124.refs_0_, bf16[2,2,64,512]{3,2,1,0:T(8,128)(2,1)S(1)} %collective-permute-done.13.refs_1_, bf16[2,2,64,512]{3,2,1,0:T(8,128)(2,1)S(1)} %collective-permute-done.14.refs_2_, ...), custom_call_target="tpu_custom_call" | custom-call | tf_op jit(solution)/shard_map/place/pallas_call | solution.py:552
  (58 shorter events, 22.8 us)
Async XLA Ops:
  0.0 16.4 %collective-permute-start = (bf16[8,2,128,512]{3,2,1,0:T(8,128)(2,1)}, bf16[8,2,128,512]{3,2,1,0:T(8,128)(2,1)S(1)}, u32[]{:S(2)}, u32[]{:S(2)}) collective-permute-start(bf16[8,2,128,512]{3,2,1,0:T(8,128)(2,1)} %own.5), channel_id=1, source_target_pairs={{0,4},{1,5},{2,6},{3,7},{4,0},{5,1},{6,2},{7,3},{8,12},{9,13},{10,... | collective-permute-start | bytes 6291464 | tf_op jit(solution)/shard_map/ppermute | solution.py:37
  4.2 8.0 %collective-permute-start.1 = (bf16[2,128,512]{2,1,0:T(8,128)(2,1)S(1)}, bf16[2,128,512]{2,1,0:T(8,128)(2,1)S(1)}, u32[]{:S(2)}, u32[]{:S(2)}) collective-permute-start(bf16[2,128,512]{2,1,0:T(8,128)(2,1)S(1)} %get-tuple-element.79), channel_id=1, source_target_pairs={{0,1},{1,2},{2,3},{3,0},{4,7},{5,4},{6,5},{7,6},{8,9},{9,10},{10,1... | collective-permute-start | bytes 786440 | tf_op jit(solution)/shard_map/ppermute | solution.py:37
  7.1 6.1 %collective-permute-start.2 = (bf16[2,128,512]{2,1,0:T(8,128)(2,1)S(1)}, bf16[2,128,512]{2,1,0:T(8,128)(2,1)S(1)}, u32[]{:S(2)}, u32[]{:S(2)}) collective-permute-start(bf16[2,128,512]{2,1,0:T(8,128)(2,1)S(1)} %get-tuple-element.80), channel_id=1, source_target_pairs={{0,7},{1,4},{2,5},{3,6},{4,1},{5,2},{6,3},{7,0},{8,15},{9,12},{10,... | collective-permute-start | bytes 786440 | tf_op jit(solution)/shard_map/ppermute | solution.py:37
  9.5 6.9 %copy-start.8 = (f32[512]{0:T(512)S(1)}, f32[512]{0:T(512)}, u32[]{:S(2)}) copy-start(f32[512]{0:T(512)} %param.11) | copy-start | bytes 6148
  9.5 6.9 %copy-start.9 = (f32[512]{0:T(512)S(1)}, f32[512]{0:T(512)}, u32[]{:S(2)}) copy-start(f32[512]{0:T(512)} %param.13) | copy-start | bytes 6148
  13.2 12.6 %collective-permute-start.3 = (bf16[6,72,512]{2,1,0:T(8,128)(2,1)S(1)}, bf16[6,72,512]{2,1,0:T(8,128)(2,1)S(1)}, u32[]{:S(2)}, u32[]{:S(2)}) collective-permute-start(bf16[6,72,512]{2,1,0:T(8,128)(2,1)S(1)} %get-tuple-element.87), channel_id=1, source_target_pairs={{0,1},{1,2},{2,3},{3,0},{4,7},{5,4},{6,5},{7,6},{8,9},{9,10},{10,1... | collective-permute-start | bytes 1327112 | tf_op jit(solution)/shard_map/ppermute | solution.py:37
  16.4 9.4 %collective-permute-start.4 = (bf16[6,72,512]{2,1,0:T(8,128)(2,1)S(1)}, bf16[6,72,512]{2,1,0:T(8,128)(2,1)S(1)}, u32[]{:S(2)}, u32[]{:S(2)}) collective-permute-start(bf16[6,72,512]{2,1,0:T(8,128)(2,1)S(1)} %get-tuple-element.88), channel_id=1, source_target_pairs={{0,7},{1,4},{2,5},{3,6},{4,1},{5,2},{6,3},{7,0},{8,15},{9,12},{10,... | collective-permute-start | bytes 1327112 | tf_op jit(solution)/shard_map/ppermute | solution.py:37
  20.2 12.4 %collective-permute-start.5 = (bf16[2,128,512]{2,1,0:T(8,128)(2,1)S(1)}, bf16[2,128,512]{2,1,0:T(8,128)(2,1)S(1)}, u32[]{:S(2)}, u32[]{:S(2)}) collective-permute-start(bf16[2,128,512]{2,1,0:T(8,128)(2,1)S(1)} %slice.3), channel_id=1, source_target_pairs={{0,8},{1,9},{2,10},{3,11},{4,12},{5,13},{6,14},{7,15},{8,16},{9,17... | collective-permute-start | bytes 786440 | tf_op jit(solution)/shard_map/ppermute | solution.py:37
  35.6 26.9 %collective-permute-start.8 = (bf16[15,64,512]{2,1,0:T(8,128)(2,1)S(1)}, bf16[15,64,512]{2,1,0:T(8,128)(2,1)S(1)}, u32[]{:S(2)}, u32[]{:S(2)}) collective-permute-start(bf16[15,64,512]{2,1,0:T(8,128)(2,1)S(1)} %get-tuple-element.104.refs_0_), channel_id=1, source_target_pairs={{0,8},{1,9},{2,10},{3,11},{4,12},{5,13},{6,14},{7,15},{8,16},{9,17... | collective-permute-start | bytes 2949128 | tf_op jit(solution)/shard_map/ppermute | solution.py:37
  35.6 8.8 %collective-permute-start.6 = (bf16[6,56,512]{2,1,0:T(8,128)(2,1)S(1)}, bf16[6,56,512]{2,1,0:T(8,128)(2,1)S(1)}, u32[]{:S(2)}, u32[]{:S(2)}) collective-permute-start(bf16[6,56,512]{2,1,0:T(8,128)(2,1)S(1)} %get-tuple-element.97), channel_id=1, source_target_pairs={{0,1},{1,2},{2,3},{3,0},{4,7},{5,4},{6,5},{7,6},{8,9},{9,10},{10,1... | collective-permute-start | bytes 1032200 | tf_op jit(solution)/shard_map/ppermute | solution.py:37
  37.4 8.4 %collective-permute-start.7 = (bf16[6,56,512]{2,1,0:T(8,128)(2,1)S(1)}, bf16[6,56,512]{2,1,0:T(8,128)(2,1)S(1)}, u32[]{:S(2)}, u32[]{:S(2)}) collective-permute-start(bf16[6,56,512]{2,1,0:T(8,128)(2,1)S(1)} %get-tuple-element.98), channel_id=1, source_target_pairs={{0,7},{1,4},{2,5},{3,6},{4,1},{5,2},{6,3},{7,0},{8,15},{9,12},{10,... | collective-permute-start | bytes 1032200 | tf_op jit(solution)/shard_map/ppermute | solution.py:37
  50.9 7.2 %collective-permute-start.10 = (bf16[15,16,512]{2,1,0:T(8,128)(2,1)S(1)}, bf16[15,16,512]{2,1,0:T(8,128)(2,1)S(1)}, u32[]{:S(2)}, u32[]{:S(2)}) collective-permute-start(bf16[15,16,512]{2,1,0:T(8,128)(2,1)S(1)} %get-tuple-element.108.refs_1_), channel_id=1, source_target_pairs={{0,24},{1,25},{2,26},{3,27},{4,28},{5,29},{6,30},{7,31},{8,0},{9,1... | collective-permute-start | bytes 737288 | tf_op jit(solution)/shard_map/ppermute | solution.py:37
  52.4 27.0 %collective-permute-start.9 = (bf16[15,48,512]{2,1,0:T(8,128)(2,1)S(1)}, bf16[15,48,512]{2,1,0:T(8,128)(2,1)S(1)}, u32[]{:S(2)}, u32[]{:S(2)}) collective-permute-start(bf16[15,48,512]{2,1,0:T(8,128)(2,1)S(1)} %get-tuple-element.107.refs_0_), channel_id=1, source_target_pairs={{0,8},{1,9},{2,10},{3,11},{4,12},{5,13},{6,14},{7,15},{8,16},{9,17... | collective-permute-start | bytes 2211848 | tf_op jit(solution)/shard_map/ppermute | solution.py:37
  52.4 10.0 %copy-start.7 = (bf16[512,512]{1,0:T(8,128)(2,1)S(1)}, bf16[512,512]{1,0:T(8,128)(2,1)}, u32[]{:S(2)}) copy-start(bf16[512,512]{1,0:T(8,128)(2,1)} %refs_4_.3) | copy-start | bytes 1572868
  58.1 10.5 %collective-permute-start.11 = (bf16[15,16,512]{2,1,0:T(8,128)(2,1)S(1)}, bf16[15,16,512]{2,1,0:T(8,128)(2,1)S(1)}, u32[]{:S(2)}, u32[]{:S(2)}) collective-permute-start(bf16[15,16,512]{2,1,0:T(8,128)(2,1)S(1)} %collective-permute-done.10), channel_id=1, source_target_pairs={{0,24},{1,25},{2,26},{3,27},{4,28},{5,29},{6,30},{7,31},{8,0},{9,1... | collective-permute-start | bytes 737288 | tf_op jit(solution)/shard_map/ppermute | solution.py:37
  68.3 21.2 %collective-permute-start.13 = (bf16[2,2,64,512]{3,2,1,0:T(8,128)(2,1)S(1)}, bf16[2,2,64,512]{3,2,1,0:T(8,128)(2,1)S(1)}, u32[]{:S(2)}, u32[]{:S(2)}) collective-permute-start(bf16[2,2,64,512]{3,2,1,0:T(8,128)(2,1)S(1)} %get-tuple-element.125), channel_id=1, source_target_pairs={{0,1},{1,2},{2,3},{3,0},{4,5},{5,6},{6,7},{7,4},{8,9},{9,10},{10,1... | collective-permute-start | bytes 786440 | tf_op jit(solution)/shard_map/ppermute | solution.py:37
  68.6 10.8 %collective-permute-start.12 = (bf16[15,16,512]{2,1,0:T(8,128)(2,1)S(1)}, bf16[15,16,512]{2,1,0:T(8,128)(2,1)S(1)}, u32[]{:S(2)}, u32[]{:S(2)}) collective-permute-start(bf16[15,16,512]{2,1,0:T(8,128)(2,1)S(1)} %collective-permute-done.11), channel_id=1, source_target_pairs={{0,24},{1,25},{2,26},{3,27},{4,28},{5,29},{6,30},{7,31},{8,32},{9,... | collective-permute-start | bytes 737288 | tf_op jit(solution)/shard_map/ppermute | solution.py:37
  68.7 22.8 %collective-permute-start.14 = (bf16[2,2,64,512]{3,2,1,0:T(8,128)(2,1)S(1)}, bf16[2,2,64,512]{3,2,1,0:T(8,128)(2,1)S(1)}, u32[]{:S(2)}, u32[]{:S(2)}) collective-permute-start(bf16[2,2,64,512]{3,2,1,0:T(8,128)(2,1)S(1)} %get-tuple-element.126), channel_id=1, source_target_pairs={{0,2},{1,3},{2,0},{3,1},{4,6},{5,7},{6,4},{7,5},{8,10},{9,11},{10,... | collective-permute-start | bytes 786440 | tf_op jit(solution)/shard_map/ppermute | solution.py:37
  72.7 18.7 %collective-permute-start.15 = (bf16[2,2,64,512]{3,2,1,0:T(8,128)(2,1)S(1)}, bf16[2,2,64,512]{3,2,1,0:T(8,128)(2,1)S(1)}, u32[]{:S(2)}, u32[]{:S(2)}) collective-permute-start(bf16[2,2,64,512]{3,2,1,0:T(8,128)(2,1)S(1)} %get-tuple-element.127), channel_id=1, source_target_pairs={{0,3},{1,0},{2,1},{3,2},{4,7},{5,4},{6,5},{7,6},{8,11},{9,8},{10,9... | collective-permute-start | bytes 786440 | tf_op jit(solution)/shard_map/ppermute | solution.py:37
  85.1 7.5 %collective-permute-start.16 = (bf16[2,2,64,512]{3,2,1,0:T(8,128)(2,1)S(1)}, bf16[2,2,64,512]{3,2,1,0:T(8,128)(2,1)S(1)}, u32[]{:S(2)}, u32[]{:S(2)}) collective-permute-start(bf16[2,2,64,512]{3,2,1,0:T(8,128)(2,1)S(1)} %get-tuple-element.131), channel_id=1, source_target_pairs={{0,1},{1,2},{2,3},{3,0},{4,5},{5,6},{6,7},{7,4},{8,9},{9,10},{10,1... | collective-permute-start | bytes 786440 | tf_op jit(solution)/shard_map/ppermute | solution.py:37
  87.3 10.5 %collective-permute-start.17 = (bf16[2,2,64,512]{3,2,1,0:T(8,128)(2,1)S(1)}, bf16[2,2,64,512]{3,2,1,0:T(8,128)(2,1)S(1)}, u32[]{:S(2)}, u32[]{:S(2)}) collective-permute-start(bf16[2,2,64,512]{3,2,1,0:T(8,128)(2,1)S(1)} %get-tuple-element.132), channel_id=1, source_target_pairs={{0,2},{1,3},{2,0},{3,1},{4,6},{5,7},{6,4},{7,5},{8,10},{9,11},{10,... | collective-permute-start | bytes 786440 | tf_op jit(solution)/shard_map/ppermute | solution.py:37
  89.5 8.3 %collective-permute-start.18 = (bf16[2,2,64,512]{3,2,1,0:T(8,128)(2,1)S(1)}, bf16[2,2,64,512]{3,2,1,0:T(8,128)(2,1)S(1)}, u32[]{:S(2)}, u32[]{:S(2)}) collective-permute-start(bf16[2,2,64,512]{3,2,1,0:T(8,128)(2,1)S(1)} %get-tuple-element.133), channel_id=1, source_target_pairs={{0,3},{1,0},{2,1},{3,2},{4,7},{5,4},{6,5},{7,6},{8,11},{9,8},{10,9... | collective-permute-start | bytes 786440 | tf_op jit(solution)/shard_map/ppermute | solution.py:37
  99.0 6.2 %collective-permute-start.20 = (bf16[4,2,64,512]{3,2,1,0:T(8,128)(2,1)S(1)}, bf16[4,2,64,512]{3,2,1,0:T(8,128)(2,1)S(1)}, u32[]{:S(2)}, u32[]{:S(2)}) collective-permute-start(bf16[4,2,64,512]{3,2,1,0:T(8,128)(2,1)S(1)} %get-tuple-element.139), channel_id=1, source_target_pairs={{0,4},{1,5},{2,6},{3,7},{4,0},{5,1},{6,2},{7,3},{8,12},{9,13},{10,... | collective-permute-start | bytes 1572872 | tf_op jit(solution)/shard_map/ppermute | solution.py:37
  103.6 2.3 %collective-permute-start.19 = (bf16[4,2,64,512]{3,2,1,0:T(8,128)(2,1)S(1)}, bf16[4,2,64,512]{3,2,1,0:T(8,128)(2,1)S(1)}, u32[]{:S(2)}, u32[]{:S(2)}) collective-permute-start(bf16[4,2,64,512]{3,2,1,0:T(8,128)(2,1)S(1)} %get-tuple-element.138), channel_id=1, source_target_pairs={{0,4},{1,5},{2,6},{3,7},{4,0},{5,1},{6,2},{7,3},{8,12},{9,13},{10,... | collective-permute-start | bytes 1572872 | tf_op jit(solution)/shard_map/ppermute | solution.py:37
  (8 other events, 33.8 us)
